TPU v7x, 256 devices: a whole 4x4x8 slice. The times are simulated.
256 devices in a mesh: gx: 16 (over z, core), gy: 4 (over y), gz: 4 (over x).
Axes of the slice: x: 4, y: 4, z: 8, core: 2. Of those that a mesh axis runs over, the one named last changes fastest.
Arguments:
- velocity: float32 [3, 128, 128, 512], P(None, 'gx', 'gy', 'gz'), may hold values from -6 to 6
- nu_tilde: float32 [128, 128, 512], P('gx', 'gy', 'gz'), may hold values from 0.05 to 2
- fluid_cells: int32 [128, 128, 512], P('gx', 'gy', 'gz'), may hold values 0 or 1
- surface: float32 [16, 4, 3, 512], P('gx', 'gz', None, 'gy'), may hold values from -64 to 64
- pitch_angle: float32 [1], replicated, may hold values from -0.15 to 0.15
- near_tiles: int32 [16, 4, 4, 8], P('gx', 'gy', 'gz'), may hold values from -1 to 31, as said below
- send_rows: int32 [16, 4, 4, 64, 128], P('gx', 'gy', 'gz'), may hold values from -1 to 32767, as said below
- ghost_cell: int32 [16, 4, 4, 2048], P('gx', 'gy', 'gz'), may hold values from 0 to 32767, as said below
- ghost_src: int32 [16, 4, 4, 8, 2048], P('gx', 'gy', 'gz'), may hold values from 0 to 8191, as said below
- ghost_weight: float32 [16, 4, 4, 8, 2048], P('gx', 'gy', 'gz'), may hold values from 0 to 1, as said below
Outputs:
- new_velocity: float32 [3, 128, 128, 512], P(None, 'gx', 'gy', 'gz')
- new_nu_tilde: float32 [128, 128, 512], P('gx', 'gy', 'gz')
- wall_distance: float32 [128, 128, 512], P('gx', 'gy', 'gz')
Inputs may be any that keep to these rules, and one draw needn't show every extreme that they name: `send_rows`: in each list of 128 slots from one device to one peer of gx+gz, live entries (local cell numbers of the sender) come first and the rest are -1. In every spanwise index some peer receives 128 live rows from every device. `ghost_src`: p * 128 + s names slot s of the rows that peer p sends to this device; it always names a live slot. `ghost_cell`: the 2048 entries of one device are distinct. `near_tiles`: distinct tiles first, the rest -1; some device lists 8 tiles. `ghost_weight`: the weights of one image point are non-negative and sum to one.
All inputs are finite; a program needn't handle non-finite values. No bound on the sum of `fluid_cells` on one device may be relied on, other than what follows from the above.
Results may differ from a plain program's by a relative error of at most 0.0003.
Values sent between devices are 32-bit elements; how exact they have to be, the bound alone decides.
No kernel may reach another device: no remote copies, remote signals or barrier semaphores. Data moves between devices by JAX's collectives and lax.ppermute only.
A program may use at most 128 MiB of HBM per device.

v0:
```python
import jax
import jax.numpy as jnp
from jax import lax
from jax.sharding import PartitionSpec as P

TY = 8


viscosity = 0.2
prod_coef = 0.1355
grad_coef = 0.622
sigma_inv = 1.5
karman = 0.41
visc_coef = 7.1
wall_coef = prod_coef / (karman * karman) + (1.0 + grad_coef) * sigma_inv
des_coef = 0.65
floor_rate = 0.3
dist_eps = 0.25
dist_cap = 8.0
time_step = 0.05


def with_halo(block, sides, width):
    for axis, dim in sides:
        count = lax.axis_size(axis)
        forward = [(i, i + 1) for i in range(count - 1)]
        backward = [(target, source) for source, target in forward]
        low = lax.ppermute(
            lax.slice_in_dim(block, block.shape[dim] - width, None, axis=dim), axis, forward
        )
        high = lax.ppermute(lax.slice_in_dim(block, 0, width, axis=dim), axis, backward)
        block = jnp.concatenate([low, block, high], axis=dim)
    return block


def rotate(points, pitch_angle):
    cosine = jnp.cos(pitch_angle[0])
    sine_value = jnp.sin(pitch_angle[0])
    turned_x = cosine * points[0] + sine_value * points[2]
    turned_z = cosine * points[2] - sine_value * points[0]
    return jnp.stack([turned_x, points[1], turned_z])


def cell_coords(tile_list, y_offset, total_span, cells_x, cells_y, cells_z):
    per_row = cells_y // TY
    slots = tile_list.shape[0]
    safe_tiles = jnp.maximum(tile_list, 0)
    plane_index = (safe_tiles // per_row).astype(jnp.float32)
    band_row = safe_tiles % per_row * TY + y_offset
    row_index = band_row[:, None] + jnp.arange(TY, dtype=jnp.int32)[None, :]
    coord_x = jnp.broadcast_to(
        (plane_index + 0.5 - 0.5 * cells_x)[:, None, None], (slots, TY, cells_z)
    )
    coord_y = jnp.broadcast_to(
        (row_index.astype(jnp.float32) + 0.5 - 0.5 * total_span)[:, :, None], (slots, TY, cells_z)
    )
    depth = jnp.arange(cells_z, dtype=jnp.int32).astype(jnp.float32) + 0.5 - 0.5 * cells_z
    coord_z = jnp.broadcast_to(depth[None, None, :], (slots, TY, cells_z))
    return jnp.stack([coord_x, coord_y, coord_z]).reshape(3, slots, TY * cells_z)


def closest(cell_list, points, nearest_sq):

    def one_slot(slot_pair):
        slot_cells, best_now = slot_pair
        step_x = slot_cells[0][:, None] - points[0][None, :]
        step_y = slot_cells[1][:, None] - points[1][None, :]
        step_z = slot_cells[2][:, None] - points[2][None, :]
        squared = step_x * step_x + step_y * step_y + step_z * step_z
        return jnp.minimum(best_now, jnp.min(squared, axis=1))

    return lax.map(one_slot, (jnp.moveaxis(cell_list, 1, 0), nearest_sq))


def place_tiles(tile_list, values, cells_x, cells_y, cells_z):
    tile_count = cells_x * (cells_y // TY)
    tile_grid = jnp.full((tile_count, TY * cells_z), dist_cap, jnp.float32)
    target = jnp.where(tile_list >= 0, tile_list, tile_count)
    tile_grid = tile_grid.at[target].set(values, mode="drop")
    return tile_grid.reshape(cells_x, cells_y, cells_z)


def neighbour(padded, direction, offset, interior):
    slices = [slice(None)]
    for dimension in range(3):
        begin = 2 + (offset if dimension == direction else 0)
        slices.append(slice(begin, begin + interior[dimension]))
    return padded[tuple(slices)]


def advance(padded, wall_dist, fluid_cells):
    interior = (padded.shape[1] - 4, padded.shape[2] - 4, padded.shape[3] - 4)
    center = neighbour(padded, 0, 0, interior)
    gradient = []
    laplace = jnp.zeros_like(center)
    for direction in range(3):
        plus_one = neighbour(padded, direction, 1, interior)
        minus_one = neighbour(padded, direction, -1, interior)
        plus_two = neighbour(padded, direction, 2, interior)
        minus_two = neighbour(padded, direction, -2, interior)
        gradient.append((minus_two - plus_two + 8.0 * (plus_one - minus_one)) / 12.0)
        laplace = laplace + (plus_one + minus_one - 2.0 * center)
    moving = center[:3]
    working = center[3]
    curl_x = gradient[1][2] - gradient[2][1]
    curl_y = gradient[2][0] - gradient[0][2]
    curl_z = gradient[0][1] - gradient[1][0]
    vort_rate = jnp.maximum(
        jnp.sqrt(curl_x * curl_x + curl_y * curl_y + curl_z * curl_z), floor_rate
    )
    positive = jnp.maximum(working, 0.0)
    chi_ratio = positive / viscosity
    chi_cubed = chi_ratio * chi_ratio * chi_ratio
    eddy_visc = positive * chi_cubed / (chi_cubed + visc_coef**3)
    diffusion = viscosity + eddy_visc
    shield_arg = diffusion / (vort_rate * karman * karman * wall_dist * wall_dist)
    shield = 1.0 - jnp.tanh((8.0 * shield_arg) ** 3)
    length = wall_dist - shield * jnp.maximum(wall_dist - des_coef, 0.0)
    convect = moving[0] * gradient[0] + moving[1] * gradient[1] + moving[2] * gradient[2]
    grad_sq = (
        gradient[0][3] * gradient[0][3]
        + gradient[1][3] * gradient[1][3]
        + gradient[2][3] * gradient[2][3]
    )
    nu_rhs = (
        -convect[3]
        + sigma_inv * ((viscosity + positive) * laplace[3] + grad_coef * grad_sq)
        + prod_coef * vort_rate * working
        - wall_coef * working * jnp.abs(working) / (length * length)
    )
    vel_rhs = -convect[:3] + diffusion[None] * laplace[:3]
    fluid_mask = fluid_cells.astype(jnp.float32)
    new_velocity = moving + time_step * fluid_mask[None] * vel_rhs
    new_nu = working + time_step * fluid_mask * nu_rhs
    return (new_velocity, new_nu)


def on_device(
    velocity,
    nu_tilde,
    fluid_cells,
    surface,
    pitch_angle,
    near_tiles,
    send_rows,
    ghost_cell,
    ghost_src,
    ghost_weight,
):
    cells_x = velocity.shape[1]
    cells_y = velocity.shape[2]
    cells_z = velocity.shape[3]
    fields = jnp.concatenate([velocity, nu_tilde[None]], axis=0)
    flat_state = fields.reshape(4, cells_x * cells_y * cells_z)
    row_list = send_rows[0, 0, 0]
    live_rows = row_list >= 0
    outgoing = jnp.where(live_rows[None], flat_state[:, jnp.where(live_rows, row_list, 0)], 0.0)
    incoming = lax.all_to_all(outgoing, ("gx", "gz"), split_axis=1, concat_axis=1, tiled=True)
    buffer = incoming.reshape(4, incoming.shape[1] * incoming.shape[2])
    values = buffer[:, ghost_src[0, 0, 0]]
    ghost_value = -jnp.sum(ghost_weight[0, 0, 0][None] * values, axis=1)
    flat_state = flat_state.at[:, ghost_cell[0, 0, 0]].set(ghost_value)
    filled = flat_state.reshape(4, cells_x, cells_y, cells_z)
    span_index = lax.axis_index("gy")
    total_span = lax.axis_size("gy") * cells_y
    tile_list = near_tiles[0, 0, 0]
    cell_list = cell_coords(tile_list, span_index * cells_y, total_span, cells_x, cells_y, cells_z)
    points = rotate(surface[0, 0], pitch_angle)
    initial = jnp.full((tile_list.shape[0], TY * cells_z), jnp.inf, jnp.float32)
    nearest_sq = closest(cell_list, lax.all_gather(points, "gy", axis=1, tiled=True), initial)
    distance = jnp.minimum(jnp.sqrt(nearest_sq + dist_eps), dist_cap)
    wall_distance = place_tiles(tile_list, distance, cells_x, cells_y, cells_z)
    padded = with_halo(filled, (("gx", 1), ("gy", 2), ("gz", 3)), 2)
    new_velocity, new_nu_tilde = advance(padded, wall_distance, fluid_cells)
    return (new_velocity, new_nu_tilde, wall_distance)


def solution(mesh):
    in_specs = (
        P(None, "gx", "gy", "gz"),
        P("gx", "gy", "gz"),
        P("gx", "gy", "gz"),
        P("gx", "gz", None, "gy"),
        P(),
        P("gx", "gy", "gz", None),
        P("gx", "gy", "gz", None, None),
        P("gx", "gy", "gz", None),
        P("gx", "gy", "gz", None, None),
        P("gx", "gy", "gz", None, None),
    )
    out_specs = (P(None, "gx", "gy", "gz"), P("gx", "gy", "gz"), P("gx", "gy", "gz"))
    return jax.shard_map(
        on_device, mesh=mesh, in_specs=in_specs, out_specs=out_specs, check_vma=False
    )
```

profile of v0, /device:TPU:32, one launch (start us, length us, event | category | flops | bytes accessed | tf_op | source)
XLA Modules:
  0.0 263.0 jit_solution(9175027282457758407)
XLA Ops:
  4.6 8.6 %copy.50 = f32[4,32768]{0,1:T(8,128)} copy(f32[4,32768]{1,0:T(4,128)S(1)} %pad_maximum_fusion.14) | data formatting | bytes 1048576 | tf_op jit(solution)/shard_map/concatenate | solution.py:153
  13.2 33.7 %gather_fusion = f32[8192,4]{1,0:T(8,128)} fusion(f32[4,32768]{0,1:T(8,128)} %copy.50, s32[8192]{0:T(1024)S(1)} %fusion.46), kind=kCustom, calls=%fused_computation | custom fusion | bytes 294912 | tf_op jit(solution)/shard_map/gather | solution.py:157
  46.9 2.8 %copy.48 = f32[64,128,4]{1,2,0:T(4,128)S(1)} copy(f32[64,128,4]{2,1,0:T(8,128)} %bitcast.131) | data formatting | bytes 262144 | tf_op jit(solution)/shard_map/gather | solution.py:157
  50.5 11.6 %all-to-all-start = ((f32[4,64,128]{2,0,1:T(4,128)}), f32[4,64,128]{2,0,1:T(4,128)S(1)}, u32[]{:S(2)}, u32[]{:S(2)}) async-start(f32[4,64,128]{2,0,1:T(4,128)} %select_bitcast_fusion), calls=%async_computation | async-start | bytes 262144 | tf_op jit(solution)/shard_map/all_to_all | solution.py:158
  63.0 11.2 %all_gather.3 = f32[3,512]{1,0:T(4,128)S(1)} all-gather(f32[3,128]{1,0:T(4,128)S(1)} %pad_maximum_fusion.19), channel_id=1, replica_groups=mesh['gx'=16,'gy'=4,'gz'=4] {'gy'}, dimensions={1}, use_global_device_ids=true | all-gather | bytes 7680 | tf_op jit(solution)/shard_map/all_gather | solution.py:170
  74.6 8.6 %while.10 = (s32[]{:T(128)}, f32[8,1024]{1,0:T(8,128)S(1)}, f32[8,3,1024]{2,0,1:T(8,128)S(1)}, f32[3,512]{1,0:T(4,128)S(1)}, s32[]{:T(128)}, /*index=5*/s32[]{:T(128)}, s32[]{}, s32[]{}) while((s32[]{:T(128)}, f32[8,1024]{1,0:T(8,128)S(1)}, f32[8,3,1024]{2,0,1:T(8,128)S(1)}, f32[3,512]{1,0:T(4,128)S(1)}, s32[]{:T(128)}, /*index=5*/s32[]{:T(128)}, ...), condition=%wide.region_4.5_spmd, body=%wide.region_2.4_spmd.sunk | while | flops 4717572 | bytes 67709 | solution.py:72
  84.6 2.7 %copy.49 = f32[4,64,128]{0,2,1:T(8,128)} copy(f32[4,64,128]{2,0,1:T(4,128)S(1)} %all-to-all-done) | data formatting | bytes 262144 | tf_op jit(solution)/shard_map/all_to_all | solution.py:158
  87.2 57.0 %gather_fusion.1 = f32[16384,4]{1,0:T(8,128)} fusion(f32[4,8192]{0,1:T(8,128)} %bitcast.129, s32[16384]{0:T(1024)S(1)} %broadcast_clamp_fusion), kind=kCustom, calls=%fused_computation.1 | custom fusion | bytes 589824 | tf_op jit(solution)/shard_map/gather | solution.py:160
  144.2 5.3 %multiply_reduce_fusion = f32[2048,4]{1,0:T(8,128)S(1)} fusion(f32[8,2048,4]{2,1,0:T(8,128)} %bitcast.130, f32[8,2048]{1,0:T(8,128)S(1)} %bitcast.148), kind=kLoop, calls=%fused_computation.15 | loop fusion | flops 122880 | bytes 360448 | tf_op jit(solution)/shard_map/reduce_sum | solution.py:161
  149.5 17.1 %scatter_custom_fusion = f32[4,32768]{0,1:T(8,128)} fusion(f32[4,32768]{0,1:T(8,128)} %copy.50, s32[2048]{0:T(1024)S(1)} %bitcast.149, f32[2048,4]{1,0:T(8,128)S(1)} %multiply_reduce_fusion), kind=kCustom, calls=%fused_computation.16 | custom fusion | flops 8192 | bytes 1572864 | tf_op jit(solution)/shard_map/scatter | solution.py:162
  166.6 10.0 %copy.51 = f32[4,8,32,128]{3,2,1,0:T(8,128)S(1)} copy(f32[4,8,32,128]{0,3,2,1:T(8,128)} %bitcast.127) | data formatting | bytes 1048576 | tf_op jit(solution)/shard_map/reshape | solution.py:163
  176.6 1.9 collective-permute-start
  178.5 3.8 %collective-permute-start.1 = (f32[4,2,32,128]{3,2,1,0:T(8,128)S(1)}, f32[4,2,32,128]{3,2,1,0:T(8,128)S(1)}, u32[]{:S(2)}, u32[]{:S(2)}) collective-permute-start(f32[4,2,32,128]{3,2,1,0:T(8,128)S(1)} %get-tuple-element.69), channel_id=1, source_target_pairs={{16,0},{32,16},{48,32},{64,48},{80,64},{96,80},{112,96},{128,112},... | collective-permute-start | bytes 393224 | tf_op jit(solution)/shard_map/ppermute | solution.py:31
  182.4 42.3 %slice_reduce_fusion = (f32[32768]{0:T(1024)}, f32[32768]{0:T(1024)}, f32[32768]{0:T(1024)}, f32[32768]{0:T(1024)}) fusion(f32[4,32768]{0,1:T(8,128)} %scatter_custom_fusion), kind=kLoop, calls=%fused_computation.8 | loop fusion | flops 98304 | bytes 1048576 | tf_op jit(solution)/shard_map/slice | solution.py:104
  224.6 10.6 %copy.61 = f32[3,8,32,128]{3,2,1,0:T(8,128)} copy(f32[3,8,32,128]{0,3,2,1:T(8,128)} %bitcast.128) | data formatting | bytes 786432 | tf_op jit(solution)/shard_map/slice | solution.py:103
  235.3 3.2 %collective-permute-start.2 = (f32[4,12,2,128]{3,2,1,0:T(2,128)S(1)}, f32[4,12,2,128]{3,2,1,0:T(2,128)S(1)}, u32[]{:S(2)}, u32[]{:S(2)}) collective-permute-start(f32[4,12,2,128]{3,2,1,0:T(2,128)S(1)} %get-tuple-element.67), channel_id=1, source_target_pairs={{0,4},{4,8},{8,12},{1,5},{5,9},{9,13},{2,6},{6,10},{10,14},{3,7},{... | collective-permute-start | bytes 147464 | tf_op jit(solution)/shard_map/ppermute | solution.py:28
  238.5 1.3 collective-permute-start.3
  241.0 3.5 %collective-permute-done.3 = f32[4,12,2,128]{3,2,1,0:T(2,128)S(1)} collective-permute-done((f32[4,12,2,128]{3,2,1,0:T(2,128)S(1)}, f32[4,12,2,128]{3,2,1,0:T(2,128)S(1)}, u32[]{:S(2)}, u32[]{:S(2)}) %collective-permute-start.3) | collective-permute-done | bytes 49184 | tf_op jit(solution)/shard_map/ppermute | solution.py:31
  245.4 3.4 %collective-permute-start.4 = (f32[4,12,36,2]{2,0,3,1:T(4,128)S(1)}, f32[4,12,36,2]{2,0,3,1:T(4,128)S(1)}, u32[]{:S(2)}, u32[]{:S(2)}) collective-permute-start(f32[4,12,36,2]{2,0,3,1:T(4,128)S(1)} %copy.56), channel_id=1, source_target_pairs={{0,1},{1,2},{2,3},{4,5},{5,6},{6,7},{8,9},{9,10},{10,11},{12,13},{... | collective-permute-start | bytes 41480 | tf_op jit(solution)/shard_map/ppermute | solution.py:28
  249.2 1.3 collective-permute-start.5
  250.7 1.3 broadcast_multiply_fusion.1
  252.5 2.8 %collective-permute-done.5 = f32[4,12,36,2]{2,0,3,1:T(4,128)} collective-permute-done((f32[4,12,36,2]{2,0,3,1:T(4,128)S(1)}, f32[4,12,36,2]{2,0,3,1:T(4,128)}, u32[]{:S(2)}, u32[]{:S(2)}) %collective-permute-start.5) | collective-permute-done | bytes 13856 | tf_op jit(solution)/shard_map/ppermute | solution.py:31
  257.8 1.5 multiply_add_fusion
  259.3 1.8 subtract_add_fusion
  (104 shorter events, 22.2 us)
Async XLA Ops:
  4.6 58.3 %copy-start.14 = (s32[1,1,1,8]{3,2,1,0:T(1,128)S(1)}, s32[1,1,1,8]{3,2,1,0:T(1,128)}, u32[]{:S(2)}) copy-start(s32[1,1,1,8]{3,2,1,0:T(1,128)} %param.17) | copy-start | bytes 100
  4.6 58.3 %copy-start.11 = (s32[1,1,1,8,2048]{4,3,2,1,0:T(8,128)S(1)}, s32[1,1,1,8,2048]{4,3,2,1,0:T(8,128)}, u32[]{:S(2)}) copy-start(s32[1,1,1,8,2048]{4,3,2,1,0:T(8,128)} %param.20) | copy-start | bytes 196612
  4.6 58.4 %copy-start.13 = (f32[1,1,3,128]{3,1,2,0:T(1,128)S(1)}, f32[1,1,3,128]{3,1,2,0:T(1,128)}, u32[]{:S(2)}) copy-start(f32[1,1,3,128]{3,1,2,0:T(1,128)} %param.15) | copy-start | bytes 4612
  4.6 79.9 %copy-start.12 = (s32[1,1,1,2048]{3,2,1,0:T(1,128)S(1)}, s32[1,1,1,2048]{3,2,1,0:T(1,128)}, u32[]{:S(2)}) copy-start(s32[1,1,1,2048]{3,2,1,0:T(1,128)} %param.19) | copy-start | bytes 24580
  13.2 131.0 %copy-start.10 = (f32[1,1,1,8,2048]{4,3,2,1,0:T(8,128)S(1)}, f32[1,1,1,8,2048]{4,3,2,1,0:T(8,128)}, u32[]{:S(2)}) copy-start(f32[1,1,1,8,2048]{4,3,2,1,0:T(8,128)} %param.21) | copy-start | bytes 196612
  50.5 34.1 %all-to-all-start = ((f32[4,64,128]{2,0,1:T(4,128)}), f32[4,64,128]{2,0,1:T(4,128)S(1)}, u32[]{:S(2)}, u32[]{:S(2)}) async-start(f32[4,64,128]{2,0,1:T(4,128)} %select_bitcast_fusion), calls=%async_computation | async-start | bytes 262144 | tf_op jit(solution)/shard_map/all_to_all | solution.py:158
  176.6 58.7 %collective-permute-start = (f32[4,2,32,128]{3,2,1,0:T(8,128)S(1)}, f32[4,2,32,128]{3,2,1,0:T(8,128)S(1)}, u32[]{:S(2)}, u32[]{:S(2)}) collective-permute-start(f32[4,2,32,128]{3,2,1,0:T(8,128)S(1)} %get-tuple-element.68), channel_id=1, source_target_pairs={{0,16},{16,32},{32,48},{48,64},{64,80},{80,96},{96,112},{112,128},... | collective-permute-start | bytes 393224 | tf_op jit(solution)/shard_map/ppermute | solution.py:28
  178.5 56.7 %collective-permute-start.1 = (f32[4,2,32,128]{3,2,1,0:T(8,128)S(1)}, f32[4,2,32,128]{3,2,1,0:T(8,128)S(1)}, u32[]{:S(2)}, u32[]{:S(2)}) collective-permute-start(f32[4,2,32,128]{3,2,1,0:T(8,128)S(1)} %get-tuple-element.69), channel_id=1, source_target_pairs={{16,0},{32,16},{48,32},{64,48},{80,64},{96,80},{112,96},{128,112},... | collective-permute-start | bytes 393224 | tf_op jit(solution)/shard_map/ppermute | solution.py:31
  235.3 16.7 %copy-start.1 = (f32[4,2,32,128]{3,2,1,0:T(8,128)}, f32[4,2,32,128]{3,2,1,0:T(8,128)S(1)}, u32[]{:S(2)}) copy-start(f32[4,2,32,128]{3,2,1,0:T(8,128)S(1)} %collective-permute-done) | copy-start | bytes 393220
  235.3 16.7 %copy-start.2 = (f32[4,2,32,128]{3,2,1,0:T(8,128)}, f32[4,2,32,128]{3,2,1,0:T(8,128)S(1)}, u32[]{:S(2)}) copy-start(f32[4,2,32,128]{3,2,1,0:T(8,128)S(1)} %collective-permute-done.1) | copy-start | bytes 393220
  235.3 5.7 %collective-permute-start.2 = (f32[4,12,2,128]{3,2,1,0:T(2,128)S(1)}, f32[4,12,2,128]{3,2,1,0:T(2,128)S(1)}, u32[]{:S(2)}, u32[]{:S(2)}) collective-permute-start(f32[4,12,2,128]{3,2,1,0:T(2,128)S(1)} %get-tuple-element.67), channel_id=1, source_target_pairs={{0,4},{4,8},{8,12},{1,5},{5,9},{9,13},{2,6},{6,10},{10,14},{3,7},{... | collective-permute-start | bytes 147464 | tf_op jit(solution)/shard_map/ppermute | solution.py:28
  238.5 6.0 %collective-permute-start.3 = (f32[4,12,2,128]{3,2,1,0:T(2,128)S(1)}, f32[4,12,2,128]{3,2,1,0:T(2,128)S(1)}, u32[]{:S(2)}, u32[]{:S(2)}) collective-permute-start(f32[4,12,2,128]{3,2,1,0:T(2,128)S(1)} %get-tuple-element.66), channel_id=1, source_target_pairs={{4,0},{8,4},{12,8},{5,1},{9,5},{13,9},{6,2},{10,6},{14,10},{7,3},{... | collective-permute-start | bytes 147464 | tf_op jit(solution)/shard_map/ppermute | solution.py:31
  244.5 7.9 %copy-start.6 = (f32[4,12,2,128]{3,2,1,0:T(2,128)}, f32[4,12,2,128]{3,2,1,0:T(2,128)S(1)}, u32[]{:S(2)}) copy-start(f32[4,12,2,128]{3,2,1,0:T(2,128)S(1)} %collective-permute-done.3) | copy-start | bytes 147460
  245.4 6.6 %collective-permute-start.4 = (f32[4,12,36,2]{2,0,3,1:T(4,128)S(1)}, f32[4,12,36,2]{2,0,3,1:T(4,128)S(1)}, u32[]{:S(2)}, u32[]{:S(2)}) collective-permute-start(f32[4,12,36,2]{2,0,3,1:T(4,128)S(1)} %copy.56), channel_id=1, source_target_pairs={{0,1},{1,2},{2,3},{4,5},{5,6},{6,7},{8,9},{9,10},{10,11},{12,13},{... | collective-permute-start | bytes 41480 | tf_op jit(solution)/shard_map/ppermute | solution.py:28
  249.2 6.1 %collective-permute-start.5 = (f32[4,12,36,2]{2,0,3,1:T(4,128)S(1)}, f32[4,12,36,2]{2,0,3,1:T(4,128)}, u32[]{:S(2)}, u32[]{:S(2)}) collective-permute-start(f32[4,12,36,2]{2,0,3,1:T(4,128)S(1)} %copy.58), channel_id=1, source_target_pairs={{1,0},{2,1},{3,2},{5,4},{6,5},{7,6},{9,8},{10,9},{11,10},{13,12},{... | collective-permute-start | bytes 41480 | tf_op jit(solution)/shard_map/ppermute | solution.py:31
  250.7 1.3 copy-start
  256.6 4.6 %copy-start.3 = (f32[4,8,32,128]{3,2,1,0:T(8,128)S(1)}, f32[4,8,32,128]{3,2,1,0:T(8,128)}, u32[]{:S(2)}) copy-start(f32[4,8,32,128]{3,2,1,0:T(8,128)} %get-tuple-element.50) | copy-start | bytes 1572868
  256.6 4.6 %copy-start.4 = (f32[4,8,32,128]{3,2,1,0:T(8,128)S(1)}, f32[4,8,32,128]{3,2,1,0:T(8,128)}, u32[]{:S(2)}) copy-start(f32[4,8,32,128]{3,2,1,0:T(8,128)} %get-tuple-element.52) | copy-start | bytes 1572868
  256.6 4.6 %copy-start.7 = (f32[32768]{0:T(1024)S(1)}, f32[32768]{0:T(1024)}, u32[]{:S(2)}) copy-start(f32[32768]{0:T(1024)} %get-tuple-element.38) | copy-start | bytes 393220
  256.6 4.6 %copy-start.8 = (f32[8,32,128]{2,1,0:T(8,128)S(1)}, f32[8,32,128]{2,1,0:T(8,128)}, u32[]{:S(2)}) copy-start(f32[8,32,128]{2,1,0:T(8,128)} %reshape.295) | copy-start | bytes 393220
  256.6 4.6 %copy-start.9 = (s32[8,32,128]{2,1,0:T(8,128)S(1)}, s32[8,32,128]{2,1,0:T(8,128)}, u32[]{:S(2)}) copy-start(s32[8,32,128]{2,1,0:T(8,128)} %param.14) | copy-start | bytes 393220
  256.6 5.5 %copy-start.5 = (f32[3,8,32,128]{3,2,1,0:T(8,128)S(1)}, f32[3,8,32,128]{3,2,1,0:T(8,128)}, u32[]{:S(2)}) copy-start(f32[3,8,32,128]{3,2,1,0:T(8,128)} %copy.61) | copy-start | bytes 1179652
where the time goes:
time: 264 us; the launch traced here: 263 us
  local copies, waits for them, and re-layouts  132 us (50%)
  other arithmetic  85.2 us (32%)
  starting transfers between devices  26.5 us (10%)
  blocking collectives  11.2 us (4%)
  waiting for transfers between devices  6.34 us (2%)
    gather x1, local copies, waits for them, and re-layouts, on_device(): values = buffer[:, ghost_src[0, 0, 0]]  57 us
    slice x1, other arithmetic, advance(): working = center[3]  42.3 us
    gather x2, local copies, waits for them, and re-layouts, on_device(): flat_state[:, jnp.where(live_rows, row_list, 0)]  36.5 us
    scatter x1, other arithmetic, on_device(): flat_state = flat_state.at[:, ghost_cell[0, 0, 0]].set(ghost_value)  17.1 us
    all_to_all x1, starting transfers between devices, on_device(): lax.all_to_all(outgoing, ('gx', 'gz'), split_axis=1, concat_axis=1, tiled...  11.6 us
    all_gather x1, blocking collectives, on_device(): lax.all_gather(points, 'gy', axis=1, tiled=True)  11.2 us
    slice x1, local copies, waits for them, and re-layouts, advance(): moving = center[:3]  10.6 us
    reshape x1, local copies, waits for them, and re-layouts, on_device(): filled = flat_state.reshape(4, cells_x, cells_y, cells_z)  10 us
  transfers between devices with their start and end apart: 7, of which 2 were waited for; matrix products, arithmetic and copies ran while one was open for 25% of the time, Pallas kernels for 0%

commit v1 on v0

v1 whole, which is shorter than its diff:
```python
import jax
import jax.numpy as jnp
from jax import lax
from jax.experimental import pallas as pl
from jax.experimental.pallas import tpu as pltpu
from jax.sharding import PartitionSpec as P

f32 = jnp.float32
bf16 = jnp.bfloat16
i32 = jnp.int32

CX, CY, CZ = 8, 32, 128
ROWS = CX * CY
TY = 8

viscosity = 0.2
prod_coef = 0.1355
grad_coef = 0.622
sigma_inv = 1.5
karman = 0.41
visc_coef = 7.1
wall_coef = prod_coef / (karman * karman) + (1.0 + grad_coef) * sigma_inv
des_coef = 0.65
floor_rate = 0.3
dist_eps = 0.25
dist_cap = 8.0
time_step = 0.05

VMEM_LIMIT = 48 * 1024 * 1024


def in_two(values):
    high = values.astype(bf16)
    return high, (values - high.astype(f32)).astype(bf16)


def one_hot(index, count):
    level = lax.broadcasted_iota(i32, (count, index.shape[1]), 0)
    return jnp.where(level == index, 1.0, 0.0).astype(bf16)


def pick_group(values, index):
    groups = values.shape[0]
    bit = 0
    while groups > 1:
        groups //= 2
        mask = ((index >> bit) & 1) == 1
        pairs = values.reshape((groups, 2) + values.shape[1:])
        values = jnp.where(mask[None], pairs[:, 1], pairs[:, 0])
        bit += 1
    return values[0]


def two_rows(ref, pair):
    return jnp.concatenate([ref[pl.ds(2 * pair, 1), :], ref[pl.ds(2 * pair + 1, 1), :]], axis=1)


def pack_kernel(vel_ref, nu_ref, rows_ref, out_ref, turn_ref, table_ref):
    for f in range(4):
        block = vel_ref[f] if f < 3 else nu_ref[...]
        for half in range(2):
            turn_ref[half, pl.ds(f, CZ, stride=4), :] = block[half * 128:half * 128 + 128].T
    for half in range(2):
        high, low = in_two(turn_ref[half])
        table_ref[:, half * 128:half * 128 + 128] = high
        table_ref[:, ROWS + half * 128:ROWS + half * 128 + 128] = low
    top = lax.broadcasted_iota(i32, (8, 128), 0) < 4

    def step(pair, carry):
        rows = two_rows(rows_ref, pair)
        hot = one_hot(rows >> 7, ROWS)
        found = jnp.dot(
            table_ref[...], jnp.concatenate([hot, hot], axis=0), preferred_element_type=f32
        )
        column = rows & 127
        both = pick_group(found.reshape(CZ // 2, 8, 256), column >> 1)
        swapped = jnp.concatenate([both[4:], both[:4]], axis=0)
        odd = (column & 1) == 1
        first = jnp.where(odd[:, :128], swapped[:, :128], both[:, :128])
        second = jnp.where(odd[:, 128:], both[:, 128:], swapped[:, 128:])
        out_ref[pl.ds(pl.multiple_of(pair * 8, 8), 8), :] = jnp.where(top, first, second)
        return carry

    lax.fori_loop(0, rows_ref.shape[0] // 2, step, 0, unroll=4)


def prepare_kernel(
    tiles_ref, place_ref, pitch_ref, s0_ref, s1_ref, s2_ref, s3_ref, vel_ref, nu_ref, cell_ref,
    base_ref, wall_ref, hot_ref, low_ref, depth_ref, span_ref
):
    for pair in range(8):
        cell = two_rows(cell_ref, pair)
        hot_ref[:, pair * 256:(pair + 1) * 256] = one_hot(cell >> 7, ROWS)
        low_ref[:, pair * 256:(pair + 1) * 256] = one_hot(cell & 127, CZ)
    count = lax.dot_general(
        hot_ref[...], low_ref[...], (((1,), (1,)), ((), ())), preferred_element_type=f32
    )
    ghost = count > 0.5
    for f in range(4):
        block = vel_ref[f] if f < 3 else nu_ref[...]
        base_ref[f] = jnp.where(ghost, 0.0, block)

    angle = jnp.full((1, 128), pitch_ref[0], f32)
    cosine = jnp.cos(angle)
    sine = jnp.sin(angle)
    turned = []
    for ref in (s0_ref, s1_ref, s2_ref, s3_ref):
        x, y, z = ref[0:1, :], ref[1:2, :], ref[2:3, :]
        turned.append((cosine * x + sine * z, y, cosine * z - sine * x))
    depth = lax.broadcasted_iota(i32, (CZ, 128), 0).astype(f32) + (0.5 - 0.5 * CZ)
    for q in range(4):
        step_z = depth - turned[q][2]
        depth_ref[q] = step_z * step_z
    wall_ref[...] = jnp.full(wall_ref.shape, dist_cap, f32)
    start = place_ref[1] * CY
    for slot in range(8):
        tile = tiles_ref[slot]

        @pl.when(tile >= 0)
        def _():
            coord_x = (tile // 4).astype(f32) + (0.5 - 0.5 * CX)
            first = (tile % 4) * TY + start
            row = lax.broadcasted_iota(i32, (8, 128), 0) + first
            coord_y = row.astype(f32) + (0.5 - 0.5 * 4 * CY)
            for q in range(4):
                step_x = coord_x - turned[q][0]
                step_y = coord_y - turned[q][1]
                span_ref[q] = step_x * step_x + step_y * step_y
            rows = []
            for r in range(8):
                least = None
                for q in range(4):
                    here = span_ref[q, r:r + 1, :] + depth_ref[q]
                    least = here if least is None else jnp.minimum(least, here)
                rows.append(jnp.min(least.T, axis=0, keepdims=True))
            nearest = jnp.concatenate(rows, axis=0)
            wall_ref[tile] = jnp.minimum(jnp.sqrt(nearest + dist_eps), dist_cap)


def fill_kernel(
    inc_ref, src_ref, weight_ref, cell_ref, base_ref,
    filled_ref, xlo_ref, xhi_ref, ylo_ref, yhi_ref, zlo_ref, zhi_ref,
    table_ref, hot_ref, value_ref, flat_ref
):
    high, low = in_two(inc_ref[...])
    table_ref[:, :CZ] = high
    table_ref[:, CZ:] = low

    def step(block, carry):
        at = pl.ds(pl.multiple_of(block * 256, 256), 256)
        total = jnp.zeros((4, 256), f32)
        for t in range(8):
            source = src_ref[t:t + 1, at]
            hot = one_hot(source & 127, CZ)
            found = jnp.dot(
                table_ref[...], jnp.concatenate([hot, hot], axis=0), preferred_element_type=f32
            )
            peer = source >> 7
            both = pick_group(found.reshape(32, 8, 256), peer >> 1)
            value = jnp.where((peer & 1) == 1, both[4:], both[:4])
            total = total + weight_ref[t:t + 1, at] * value
        total = -total
        cell = two_rows(cell_ref, block)
        hot = one_hot(cell >> 7, ROWS)
        put = pl.multiple_of(block * 512, 512)
        hot_ref[:, pl.ds(put, 256)] = hot
        hot_ref[:, pl.ds(put + 256, 256)] = hot
        here = lax.broadcasted_iota(i32, (CZ, 256), 0) == (cell & 127)
        rest = total - total.astype(bf16).astype(f32)
        for f in range(4):
            value_ref[pl.ds(f * CZ, CZ), pl.ds(put, 256)] = jnp.where(
                here, total[f:f + 1], 0.0).astype(bf16)
            value_ref[pl.ds(f * CZ, CZ), pl.ds(put + 256, 256)] = jnp.where(
                here, rest[f:f + 1], 0.0).astype(bf16)
        return carry

    lax.fori_loop(0, 8, step, 0)
    added = lax.dot_general(
        hot_ref[...], value_ref[...], (((1,), (1,)), ((), ())), preferred_element_type=f32
    )
    for f in range(4):
        block = base_ref[f] + added[:, f * CZ:(f + 1) * CZ]
        filled_ref[f] = block
        flat_ref[pl.ds(f * ROWS, ROWS), :] = block
        xlo_ref[pl.ds(f * 64, 64), :] = block[:64]
        xhi_ref[pl.ds(f * 64, 64), :] = block[ROWS - 64:]
    for h in range(2):
        ylo_ref[pl.ds(h * 32, 32), :] = flat_ref[pl.ds(h, 32, stride=32), :]
        yhi_ref[pl.ds(h * 32, 32), :] = flat_ref[pl.ds(30 + h, 32, stride=32), :]
    for b in range(8):
        turn = flat_ref[pl.ds(b * 128, 128), :].T
        zlo_ref[pl.ds(b * 2, 2), :] = turn[0:2]
        zhi_ref[pl.ds(b * 2, 2), :] = turn[126:128]


def advance_kernel(
    place_ref, filled_ref, xlo_ref, xhi_ref, ylo_ref, yhi_ref, zlo_ref, zhi_ref, wall_ref, fluid_ref,
    vel_ref, nu_ref, pad_ref, edge_ref
):
    ix, iy, iz = place_ref[0], place_ref[1], place_ref[2]
    keep = lambda flag, value: jnp.where(flag, value, 0.0)
    for f in range(4):
        pad_ref[f, 2:10, 8:40, :] = filled_ref[f].reshape(8, 32, 128)
        pad_ref[f, 0:2, 8:40, :] = keep(ix > 0, xlo_ref[f * 64:(f + 1) * 64, :]).reshape(2, 32, 128)
        pad_ref[f, 10:12, 8:40, :] = keep(ix < 15, xhi_ref[f * 64:(f + 1) * 64, :]).reshape(2, 32, 128)
    for h in range(2):
        low = keep(iy > 0, ylo_ref[h * 32:(h + 1) * 32, :])
        high = keep(iy < 3, yhi_ref[h * 32:(h + 1) * 32, :])
        for f in range(4):
            for i in range(8):
                n = f * 8 + i
                pad_ref[f, 2 + i, 6 + h:7 + h, :] = low[n:n + 1]
                pad_ref[f, 2 + i, 40 + h:41 + h, :] = high[n:n + 1]
    zlow = keep(iz > 0, zlo_ref[...])
    zhigh = keep(iz < 3, zhi_ref[...])
    for b in range(8):
        block = jnp.concatenate(
            [zhigh[2 * b:2 * b + 2], jnp.zeros((124, 128), f32), zlow[2 * b:2 * b + 2]], axis=0
        )
        edge_ref[b // 2, (b % 2) * 4:(b % 2) * 4 + 4] = block.T.reshape(4, 32, 128)

    lane = lax.broadcasted_iota(i32, (8, 128), 1)

    def plane(i, carry):
        for c in range(4):
            j = 8 + 8 * c
            center, grads, laps = [], [], []
            for f in range(4):
                mid = pad_ref[f, i + 2, j:j + 8, :]
                edge = edge_ref[f, i, 8 * c:8 * c + 8, :]
                xs = [pad_ref[f, i + 2 + h, j:j + 8, :] for h in (-2, -1, 1, 2)]
                ys = [pad_ref[f, i + 2, j + h:j + 8 + h, :] for h in (-2, -1, 1, 2)]
                zs = [
                    pltpu.roll(jnp.where(lane >= 126, edge, mid), 2, 1),
                    pltpu.roll(jnp.where(lane >= 127, edge, mid), 1, 1),
                    pltpu.roll(jnp.where(lane < 1, edge, mid), 127, 1),
                    pltpu.roll(jnp.where(lane < 2, edge, mid), 126, 1),
                ]
                center.append(mid)
                grads.append([
                    ((m2 - p2) + 8.0 * (p1 - m1)) * (1.0 / 12.0) for m2, m1, p1, p2 in (xs, ys, zs)
                ])
                around = (xs[1] + xs[2]) + (ys[1] + ys[2]) + (zs[1] + zs[2])
                laps.append(around - 6.0 * mid)
            u, v, w, working = center
            curl_x = grads[2][1] - grads[1][2]
            curl_y = grads[0][2] - grads[2][0]
            curl_z = grads[1][0] - grads[0][1]
            rate = jnp.maximum(
                jnp.sqrt(curl_x * curl_x + curl_y * curl_y + curl_z * curl_z), floor_rate
            )
            positive = jnp.maximum(working, 0.0)
            chi = positive * (1.0 / viscosity)
            cubed = chi * chi * chi
            diffusion = viscosity + positive * cubed / (cubed + visc_coef**3)
            wall = wall_ref[i, 8 * c:8 * c + 8, :]
            arg = 8.0 * (diffusion / (rate * (karman * karman) * wall * wall))
            shield = 1.0 - jnp.tanh(arg * arg * arg)
            length = wall - shield * jnp.maximum(wall - des_coef, 0.0)
            convect = [u * g[0] + v * g[1] + w * g[2] for g in grads]
            gn = grads[3]
            grad_sq = gn[0] * gn[0] + gn[1] * gn[1] + gn[2] * gn[2]
            nu_rhs = (
                sigma_inv * ((viscosity + positive) * laps[3] + grad_coef * grad_sq)
                - convect[3]
                + prod_coef * rate * working
                - wall_coef * working * jnp.abs(working) / (length * length)
            )
            mask = fluid_ref[i, 8 * c:8 * c + 8, :].astype(f32) * time_step
            for f in range(3):
                vel_ref[f, i, 8 * c:8 * c + 8, :] = center[f] + mask * (diffusion * laps[f] - convect[f])
            nu_ref[i, 8 * c:8 * c + 8, :] = working + mask * nu_rhs
        return carry

    lax.fori_loop(0, 8, plane, 0)


def vmem():
    return pl.BlockSpec(memory_space=pltpu.VMEM)


def smem():
    return pl.BlockSpec(memory_space=pltpu.SMEM)


def call(kernel, out_shape, in_specs, scratch, name, flops, moved):
    many = isinstance(out_shape, (list, tuple))
    return pl.pallas_call(
        kernel,
        out_shape=out_shape,
        in_specs=in_specs,
        out_specs=[vmem()] * len(out_shape) if many else vmem(),
        scratch_shapes=scratch,
        compiler_params=pltpu.CompilerParams(vmem_limit_bytes=VMEM_LIMIT),
        cost_estimate=pl.CostEstimate(flops=flops, bytes_accessed=moved, transcendentals=0),
        name=name,
    )


def ring(block, axis, shift):
    count = lax.axis_size(axis)
    return lax.ppermute(block, axis, [(i, (i + shift) % count) for i in range(count)])


def on_device(
    velocity, nu_tilde, fluid_cells, surface, pitch_angle, near_tiles, send_rows, ghost_cell,
    ghost_src, ghost_weight,
):
    shape = lambda *dims, dtype=f32: jax.ShapeDtypeStruct(dims, dtype)
    vel = velocity.reshape(3, ROWS, CZ)
    nu = nu_tilde.reshape(ROWS, CZ)
    cells = ghost_cell.reshape(16, 128)
    place = jnp.stack([lax.axis_index("gx"), lax.axis_index("gy"), lax.axis_index("gz")]).astype(i32)
    own = surface.reshape(3, 128)
    others = [ring(own, "gy", d) for d in (1, 2, 3)]

    outgoing = call(
        pack_kernel, shape(256, 128), [vmem()] * 3,
        [pltpu.VMEM((2, 512, 128), f32), pltpu.VMEM((512, 2 * ROWS), bf16)],
        "pack_rows", 4_000_000_000, 1_000_000,
    )(vel, nu, send_rows.reshape(64, 128))
    incoming = lax.all_to_all(
        outgoing.reshape(256 * 128), ("gx", "gz"), split_axis=0, concat_axis=0, tiled=True
    ).reshape(256, 128)

    base, wall = call(
        prepare_kernel, (shape(4, ROWS, CZ), shape(32, TY, CZ)),
        [smem()] * 3 + [vmem()] * 7,
        [pltpu.VMEM((ROWS, 2048), bf16), pltpu.VMEM((CZ, 2048), bf16),
         pltpu.VMEM((4, CZ, 128), f32), pltpu.VMEM((4, 8, 128), f32)],
        "prepare", 200_000_000, 2_000_000,
    )(near_tiles.reshape(8), place, pitch_angle, own, *others, vel, nu, cells)

    filled, xlo, xhi, ylo, yhi, zlo, zhi = call(
        fill_kernel,
        (shape(4, ROWS, CZ), shape(256, 128), shape(256, 128), shape(64, 128), shape(64, 128),
         shape(16, 128), shape(16, 128)),
        [vmem()] * 5,
        [pltpu.VMEM((256, 256), bf16), pltpu.VMEM((ROWS, 4096), bf16),
         pltpu.VMEM((512, 4096), bf16), pltpu.VMEM((4 * ROWS, CZ), f32)],
        "fill_ghosts", 4_000_000_000, 2_000_000,
    )(incoming, ghost_src.reshape(8, 2048), ghost_weight.reshape(8, 2048), cells, base)

    from_below = [ring(xhi, "gx", 1), ring(yhi, "gy", 1), ring(zhi, "gz", 1)]
    from_above = [ring(xlo, "gx", -1), ring(ylo, "gy", -1), ring(zlo, "gz", -1)]
    wall = wall.reshape(CX, CY, CZ)
    new_velocity, new_nu = call(
        advance_kernel, (shape(3, CX, CY, CZ), shape(CX, CY, CZ)),
        [smem()] + [vmem()] * 9,
        [pltpu.VMEM((4, 12, 48, CZ), f32), pltpu.VMEM((4, CX, CY, CZ), f32)],
        "advance", 20_000_000, 3_000_000,
    )(place, filled, from_below[0], from_above[0], from_below[1], from_above[1],
      from_below[2], from_above[2], wall, fluid_cells)
    return new_velocity, new_nu, wall


def solution(mesh):
    in_specs = (
        P(None, "gx", "gy", "gz"),
        P("gx", "gy", "gz"),
        P("gx", "gy", "gz"),
        P("gx", "gz", None, "gy"),
        P(),
        P("gx", "gy", "gz", None),
        P("gx", "gy", "gz", None, None),
        P("gx", "gy", "gz", None),
        P("gx", "gy", "gz", None, None),
        P("gx", "gy", "gz", None, None),
    )
    out_specs = (P(None, "gx", "gy", "gz"), P("gx", "gy", "gz"), P("gx", "gy", "gz"))
    return jax.shard_map(
        on_device, mesh=mesh, in_specs=in_specs, out_specs=out_specs, check_vma=False
    )
```

time: 264 us -> 59.4 us (0.23)
  the two profiles are of different devices: /device:TPU:32 before, /device:TPU:6 now
where the time goes in v1:
time: 59.4 us
  starting transfers between devices  23 us (39%)
  Pallas kernels  20 us (34%)
  waiting for transfers between devices  11.6 us (20%)
  local copies, waits for them, and re-layouts  3.33 us (6%)
  between operations  1.4 us (2%)
    all_to_all x1, starting transfers between devices, on_device(): lax.all_to_all(outgoing.reshape(256 * 128), ('gx', 'gz'), split_axis=0, c...  12.1 us
    ppermute x9, waiting for transfers between devices, ring(): lax.ppermute(block, axis, [(i, (i + shift) % count) for i in range(count)])  11.6 us
    ppermute x9, starting transfers between devices, ring(): lax.ppermute(block, axis, [(i, (i + shift) % count) for i in range(count)])  10.9 us
    pallas_call x1, Pallas kernels, on_device(): call(pack_kernel, shape(256, 128), [vmem()] * 3, [pltpu.VMEM((2, 512, 128...  6.96 us
    pallas_call x1, Pallas kernels, on_device(): call(fill_kernel, (shape(4, ROWS, CZ), shape(256, 128), shape(256, 128),...  6.83 us
    pallas_call x1, Pallas kernels, on_device(): call(prepare_kernel, (shape(4, ROWS, CZ), shape(32, TY, CZ)), [smem()] *...  3.37 us
    unnamed x25, local copies, waits for them, and re-layouts  3.33 us
    pallas_call x1, Pallas kernels, on_device(): call(advance_kernel, (shape(3, CX, CY, CZ), shape(CX, CY, CZ)), [smem()]...  2.85 us
  transfers between devices with their start and end apart: 10, of which 4 were waited for; matrix products, arithmetic and copies ran while one was open for 0% of the time, Pallas kernels for 6%

profile of v1, /device:TPU:6, one launch (start us, length us, event | category | flops | bytes accessed | tf_op | source)
XLA Modules:
  0.0 59.4 jit_solution(5613661694281017179)
XLA Ops:
  0.6 1.0 %copy-done.2 = f32[3,8,32,128]{3,2,1,0:T(8,128)S(1)} copy-done((f32[3,8,32,128]{3,2,1,0:T(8,128)S(1)}, f32[3,8,32,128]{3,2,1,0:T(8,128)}, u32[]{:S(2)}) %copy-start.2) | copy-done | bytes 393240
  1.6 0.9 %copy-done.4 = f32[8,32,128]{2,1,0:T(8,128)S(1)} copy-done((f32[8,32,128]{2,1,0:T(8,128)S(1)}, f32[8,32,128]{2,1,0:T(8,128)}, u32[]{:S(2)}) %copy-start.4) | copy-done | bytes 131096
  2.5 0.8 %copy-done.8 = s32[1,1,1,64,128]{4,3,2,1,0:T(8,128)S(1)} copy-done((s32[1,1,1,64,128]{4,3,2,1,0:T(8,128)S(1)}, s32[1,1,1,64,128]{4,3,2,1,0:T(8,128)}, u32[]{:S(2)}) %copy-start.8) | copy-done | bytes 32792
  3.3 7.0 %pack_rows.1 = f32[256,128]{1,0:T(8,128)} custom-call(f32[3,256,128]{2,1,0:T(8,128)S(1)} %bitcast.23, f32[256,128]{1,0:T(8,128)S(1)} %bitcast.25, s32[64,128]{1,0:T(8,128)S(1)} %bitcast.29), custom_call_target="tpu_custom_call" | custom-call | flops 4000000000 | bytes 1000000 | tf_op jit(solution)/shard_map/pack_rows/pallas_call | solution.py:317
  10.3 12.1 %all-to-all-start = ((f32[64,512,1]{1,2,0:T(1,128)}), f32[64,512,1]{1,2,0:T(1,128)S(1)}, u32[]{:S(2)}, u32[]{:S(2)}) async-start(f32[64,512,1]{1,2,0:T(1,128)} %bitcast.6), calls=%async_computation | async-start | bytes 262144 | tf_op jit(solution)/shard_map/all_to_all | solution.py:322
  22.4 3.1 %collective-permute-start.2 = (f32[3,128]{1,0:T(4,128)S(1)}, f32[3,128]{1,0:T(4,128)S(1)}, u32[]{:S(2)}, u32[]{:S(2)}) collective-permute-start(f32[3,128]{1,0:T(4,128)S(1)} %bitcast.19), channel_id=1, source_target_pairs={{0,12},{4,0},{8,4},{12,8},{1,13},{5,1},{9,5},{13,9},{2,14},{6,2},{... | collective-permute-start | bytes 4616 | tf_op jit(solution)/shard_map/ppermute | solution.py:302
  25.5 0.6 %collective-permute-start.1 = (f32[3,128]{1,0:T(4,128)S(1)}, f32[3,128]{1,0:T(4,128)S(1)}, u32[]{:S(2)}, u32[]{:S(2)}) collective-permute-start(f32[3,128]{1,0:T(4,128)S(1)} %bitcast.20), channel_id=1, source_target_pairs={{0,8},{4,12},{8,0},{12,4},{1,9},{5,13},{9,1},{13,5},{2,10},{6,14},... | collective-permute-start | bytes 4616 | tf_op jit(solution)/shard_map/ppermute | solution.py:302
  26.1 1.0 %collective-permute-start = (f32[3,128]{1,0:T(4,128)S(1)}, f32[3,128]{1,0:T(4,128)S(1)}, u32[]{:S(2)}, u32[]{:S(2)}) collective-permute-start(f32[3,128]{1,0:T(4,128)S(1)} %bitcast.21), channel_id=1, source_target_pairs={{0,4},{4,8},{8,12},{12,0},{1,5},{5,9},{9,13},{13,1},{2,6},{6,10},{... | collective-permute-start | bytes 4616 | tf_op jit(solution)/shard_map/ppermute | solution.py:302
  27.1 0.1 pad_add_fusion.place_ref
  27.8 2.7 %collective-permute-done.1.s2_ref = f32[3,128]{1,0:T(4,128)S(1)} collective-permute-done((f32[3,128]{1,0:T(4,128)S(1)}, f32[3,128]{1,0:T(4,128)S(1)}, u32[]{:S(2)}, u32[]{:S(2)}) %collective-permute-start.1) | collective-permute-done | bytes 1568 | tf_op jit(solution)/shard_map/ppermute | solution.py:302
  30.6 0.3 collective-permute-done.s1_ref
  30.9 0.6 %copy-done.10 = s32[1,1,1,8]{3,2,1,0:T(1,128)S(1)} copy-done((s32[1,1,1,8]{3,2,1,0:T(1,128)S(1)}, s32[1,1,1,8]{3,2,1,0:T(1,128)}, u32[]{:S(2)}) %copy-start.10) | copy-done | bytes 56
  31.6 3.4 %prepare.1 = (f32[4,256,128]{2,1,0:T(8,128)S(1)}, f32[32,8,128]{2,1,0:T(8,128)}) custom-call(s32[8]{0:T(128)S(1)} %bitcast.32, s32[3]{0:T(128)S(1)} %pad_add_fusion.place_ref, f32[1]{0:T(128)S(6)} %copy.17.pitch_ref, f32[3,128]{1,0:T(4,128)S(1)} %bitcast.22, f32[3,128]{1,0:T(4,128)S(1)} %collective-permute-done.s1_ref, ...), custom_call_target="tpu_custom_call" | custom-call | flops 200000000 | bytes 2000000 | tf_op jit(solution)/shard_map/prepare/pallas_call | solution.py:326
  34.9 0.0 all-to-all-done
  34.9 0.0 copy-start
  34.9 0.0 copy-start.1
  35.0 6.8 %fill_ghosts.1 = (f32[4,256,128]{2,1,0:T(8,128)S(1)}, f32[256,128]{1,0:T(8,128)S(1)}, f32[256,128]{1,0:T(8,128)S(1)}, f32[64,128]{1,0:T(8,128)S(1)}, f32[64,128]...) custom-call(f32[256,128]{1,0:T(8,128)S(1)} %bitcast.16, s32[8,2048]{1,0:T(8,128)S(1)} %bitcast.27, ...), custom_call_target="tpu_custom_call" | custom-call | flops 4000000000 | bytes 2000000 | tf_op jit(solution)/shard_map/fill_ghosts/pallas_call | solution.py:334
  41.8 0.0 collective-permute-start.3
  41.8 3.0 %collective-permute-start.4 = (f32[256,128]{1,0:T(8,128)S(1)}, f32[256,128]{1,0:T(8,128)S(1)}, u32[]{:S(2)}, u32[]{:S(2)}) collective-permute-start(f32[256,128]{1,0:T(8,128)S(1)} %get-tuple-element.17), channel_id=1, source_target_pairs={{0,240},{16,0},{32,16},{48,32},{64,48},{80,64},{96,80},{112,96},{1... | collective-permute-start | bytes 393224 | tf_op jit(solution)/shard_map/ppermute | solution.py:302
  44.8 0.0 collective-permute-start.5
  44.8 3.2 %collective-permute-start.6 = (f32[64,128]{1,0:T(8,128)S(1)}, f32[64,128]{1,0:T(8,128)S(1)}, u32[]{:S(2)}, u32[]{:S(2)}) collective-permute-start(f32[64,128]{1,0:T(8,128)S(1)} %get-tuple-element.19), channel_id=1, source_target_pairs={{0,12},{4,0},{8,4},{12,8},{1,13},{5,1},{9,5},{13,9},{2,14},{6,2},{... | collective-permute-start | bytes 98312 | tf_op jit(solution)/shard_map/ppermute | solution.py:302
  48.0 3.6 %collective-permute-done.7.zlo_ref = f32[16,128]{1,0:T(8,128)S(1)} collective-permute-done((f32[16,128]{1,0:T(8,128)S(1)}, f32[16,128]{1,0:T(8,128)S(1)}, u32[]{:S(2)}, u32[]{:S(2)}) %collective-permute-start.7) | collective-permute-done | bytes 8224 | tf_op jit(solution)/shard_map/ppermute | solution.py:302
  51.7 4.9 %collective-permute-done.8.zhi_ref = f32[16,128]{1,0:T(8,128)S(1)} collective-permute-done((f32[16,128]{1,0:T(8,128)S(1)}, f32[16,128]{1,0:T(8,128)S(1)}, u32[]{:S(2)}, u32[]{:S(2)}) %collective-permute-start.8) | collective-permute-done | bytes 8224 | tf_op jit(solution)/shard_map/ppermute | solution.py:302
  56.6 2.8 %advance.1 = (f32[3,8,32,128]{3,2,1,0:T(8,128)}, f32[8,32,128]{2,1,0:T(8,128)}) custom-call(s32[3]{0:T(128)S(1)} %pad_add_fusion.place_ref, f32[4,256,128]{2,1,0:T(8,128)S(1)} %get-tuple-element.15.filled_ref, f32[256,128]{1,0:T(8,128)S(1)} %collective-permute-done.3.xlo_ref, f32[256,128]{1,0:T(8,128)S(1)} %collective-permute-done.4.xhi_ref, ...), custom_call_target="tpu_custom_call" | custom-call | flops 20000000 | bytes 3000000 | tf_op jit(solution)/shard_map/advance/pallas_call | solution.py:347
  (26 shorter events, 0.1 us)
Async XLA Ops:
  0.6 1.0 %copy-start.2 = (f32[3,8,32,128]{3,2,1,0:T(8,128)S(1)}, f32[3,8,32,128]{3,2,1,0:T(8,128)}, u32[]{:S(2)}) copy-start(f32[3,8,32,128]{3,2,1,0:T(8,128)} %param.10) | copy-start | bytes 1179652
  1.6 0.9 %copy-start.4 = (f32[8,32,128]{2,1,0:T(8,128)S(1)}, f32[8,32,128]{2,1,0:T(8,128)}, u32[]{:S(2)}) copy-start(f32[8,32,128]{2,1,0:T(8,128)} %param.11) | copy-start | bytes 393220
  2.5 0.8 %copy-start.8 = (s32[1,1,1,64,128]{4,3,2,1,0:T(8,128)S(1)}, s32[1,1,1,64,128]{4,3,2,1,0:T(8,128)}, u32[]{:S(2)}) copy-start(s32[1,1,1,64,128]{4,3,2,1,0:T(8,128)} %param.16) | copy-start | bytes 98308
  3.3 27.6 %copy-start.3 = (f32[3,8,32,128]{3,2,1,0:T(8,128)S(1)}, f32[3,8,32,128]{3,2,1,0:T(8,128)}, u32[]{:S(2)}) copy-start(f32[3,8,32,128]{3,2,1,0:T(8,128)} %param.10) | copy-start | bytes 1179652
  10.2 12.1 %copy-start.11 = (f32[1,1,3,128]{3,1,2,0:T(1,128)S(1)}, f32[1,1,3,128]{3,1,2,0:T(1,128)}, u32[]{:S(2)}) copy-start(f32[1,1,3,128]{3,1,2,0:T(1,128)} %param.13) | copy-start | bytes 4612
  10.3 20.6 %copy-start.5 = (f32[8,32,128]{2,1,0:T(8,128)S(1)}, f32[8,32,128]{2,1,0:T(8,128)}, u32[]{:S(2)}) copy-start(f32[8,32,128]{2,1,0:T(8,128)} %param.11) | copy-start | bytes 393220
  10.3 24.7 %all-to-all-start = ((f32[64,512,1]{1,2,0:T(1,128)}), f32[64,512,1]{1,2,0:T(1,128)S(1)}, u32[]{:S(2)}, u32[]{:S(2)}) async-start(f32[64,512,1]{1,2,0:T(1,128)} %bitcast.6), calls=%async_computation | async-start | bytes 262144 | tf_op jit(solution)/shard_map/all_to_all | solution.py:322
  22.4 5.4 %collective-permute-start.2 = (f32[3,128]{1,0:T(4,128)S(1)}, f32[3,128]{1,0:T(4,128)S(1)}, u32[]{:S(2)}, u32[]{:S(2)}) collective-permute-start(f32[3,128]{1,0:T(4,128)S(1)} %bitcast.19), channel_id=1, source_target_pairs={{0,12},{4,0},{8,4},{12,8},{1,13},{5,1},{9,5},{13,9},{2,14},{6,2},{... | collective-permute-start | bytes 4616 | tf_op jit(solution)/shard_map/ppermute | solution.py:302
  25.5 5.1 %collective-permute-start.1 = (f32[3,128]{1,0:T(4,128)S(1)}, f32[3,128]{1,0:T(4,128)S(1)}, u32[]{:S(2)}, u32[]{:S(2)}) collective-permute-start(f32[3,128]{1,0:T(4,128)S(1)} %bitcast.20), channel_id=1, source_target_pairs={{0,8},{4,12},{8,0},{12,4},{1,9},{5,13},{9,1},{13,5},{2,10},{6,14},... | collective-permute-start | bytes 4616 | tf_op jit(solution)/shard_map/ppermute | solution.py:302
  26.1 4.8 %collective-permute-start = (f32[3,128]{1,0:T(4,128)S(1)}, f32[3,128]{1,0:T(4,128)S(1)}, u32[]{:S(2)}, u32[]{:S(2)}) collective-permute-start(f32[3,128]{1,0:T(4,128)S(1)} %bitcast.21), channel_id=1, source_target_pairs={{0,4},{4,8},{8,12},{12,0},{1,5},{5,9},{9,13},{13,1},{2,6},{6,10},{... | collective-permute-start | bytes 4616 | tf_op jit(solution)/shard_map/ppermute | solution.py:302
  27.1 3.8 %copy-start.9 = (s32[1,1,1,2048]{3,2,1,0:T(1,128)S(1)}, s32[1,1,1,2048]{3,2,1,0:T(1,128)}, u32[]{:S(2)}) copy-start(s32[1,1,1,2048]{3,2,1,0:T(1,128)} %param.17) | copy-start | bytes 24580
  30.9 0.7 %copy-start.10 = (s32[1,1,1,8]{3,2,1,0:T(1,128)S(1)}, s32[1,1,1,8]{3,2,1,0:T(1,128)}, u32[]{:S(2)}) copy-start(s32[1,1,1,8]{3,2,1,0:T(1,128)} %param.15) | copy-start | bytes 100
  31.6 3.4 %copy-start.6 = (s32[1,1,1,8,2048]{4,3,2,1,0:T(8,128)S(1)}, s32[1,1,1,8,2048]{4,3,2,1,0:T(8,128)}, u32[]{:S(2)}) copy-start(s32[1,1,1,8,2048]{4,3,2,1,0:T(8,128)} %param.18) | copy-start | bytes 196612
  31.6 3.4 %copy-start.7 = (f32[1,1,1,8,2048]{4,3,2,1,0:T(8,128)S(1)}, f32[1,1,1,8,2048]{4,3,2,1,0:T(8,128)}, u32[]{:S(2)}) copy-start(f32[1,1,1,8,2048]{4,3,2,1,0:T(8,128)} %param.19) | copy-start | bytes 196612
  34.9 21.6 %copy-start = (s32[8,32,128]{2,1,0:T(8,128)S(1)}, s32[8,32,128]{2,1,0:T(8,128)}, u32[]{:S(2)}) copy-start(s32[8,32,128]{2,1,0:T(8,128)} %fluid_ref.1) | copy-start | bytes 393220
  34.9 21.6 %copy-start.1 = (f32[32,8,128]{2,1,0:T(8,128)S(1)}, f32[32,8,128]{2,1,0:T(8,128)}, u32[]{:S(2)}) copy-start(f32[32,8,128]{2,1,0:T(8,128)} %get-tuple-element.22) | copy-start | bytes 393220
  41.8 14.7 %collective-permute-start.3 = (f32[256,128]{1,0:T(8,128)S(1)}, f32[256,128]{1,0:T(8,128)S(1)}, u32[]{:S(2)}, u32[]{:S(2)}) collective-permute-start(f32[256,128]{1,0:T(8,128)S(1)} %get-tuple-element.16), channel_id=1, source_target_pairs={{0,16},{16,32},{32,48},{48,64},{64,80},{80,96},{96,112},{112,128},... | collective-permute-start | bytes 393224 | tf_op jit(solution)/shard_map/ppermute | solution.py:302
  41.8 14.7 %collective-permute-start.4 = (f32[256,128]{1,0:T(8,128)S(1)}, f32[256,128]{1,0:T(8,128)S(1)}, u32[]{:S(2)}, u32[]{:S(2)}) collective-permute-start(f32[256,128]{1,0:T(8,128)S(1)} %get-tuple-element.17), channel_id=1, source_target_pairs={{0,240},{16,0},{32,16},{48,32},{64,48},{80,64},{96,80},{112,96},{1... | collective-permute-start | bytes 393224 | tf_op jit(solution)/shard_map/ppermute | solution.py:302
  44.8 11.8 %collective-permute-start.5 = (f32[64,128]{1,0:T(8,128)S(1)}, f32[64,128]{1,0:T(8,128)S(1)}, u32[]{:S(2)}, u32[]{:S(2)}) collective-permute-start(f32[64,128]{1,0:T(8,128)S(1)} %get-tuple-element.18), channel_id=1, source_target_pairs={{0,4},{4,8},{8,12},{12,0},{1,5},{5,9},{9,13},{13,1},{2,6},{6,10},{... | collective-permute-start | bytes 98312 | tf_op jit(solution)/shard_map/ppermute | solution.py:302
  44.8 11.8 %collective-permute-start.6 = (f32[64,128]{1,0:T(8,128)S(1)}, f32[64,128]{1,0:T(8,128)S(1)}, u32[]{:S(2)}, u32[]{:S(2)}) collective-permute-start(f32[64,128]{1,0:T(8,128)S(1)} %get-tuple-element.19), channel_id=1, source_target_pairs={{0,12},{4,0},{8,4},{12,8},{1,13},{5,1},{9,5},{13,9},{2,14},{6,2},{... | collective-permute-start | bytes 98312 | tf_op jit(solution)/shard_map/ppermute | solution.py:302
  48.0 3.7 %collective-permute-start.7 = (f32[16,128]{1,0:T(8,128)S(1)}, f32[16,128]{1,0:T(8,128)S(1)}, u32[]{:S(2)}, u32[]{:S(2)}) collective-permute-start(f32[16,128]{1,0:T(8,128)S(1)} %get-tuple-element.20), channel_id=1, source_target_pairs={{0,1},{1,2},{2,3},{3,0},{4,5},{5,6},{6,7},{7,4},{8,9},{9,10},{10,1... | collective-permute-start | bytes 24584 | tf_op jit(solution)/shard_map/ppermute | solution.py:302
  51.7 4.9 %collective-permute-start.8 = (f32[16,128]{1,0:T(8,128)S(1)}, f32[16,128]{1,0:T(8,128)S(1)}, u32[]{:S(2)}, u32[]{:S(2)}) collective-permute-start(f32[16,128]{1,0:T(8,128)S(1)} %get-tuple-element.21), channel_id=1, source_target_pairs={{0,3},{1,0},{2,1},{3,2},{4,7},{5,4},{6,5},{7,6},{8,11},{9,8},{10,9... | collective-permute-start | bytes 24584 | tf_op jit(solution)/shard_map/ppermute | solution.py:302

commit v2 on v1

--- a/solution.py
+++ b/solution.py
@@ -55,8 +55,20 @@
     return jnp.concatenate([ref[pl.ds(2 * pair, 1), :], ref[pl.ds(2 * pair + 1, 1), :]], axis=1)
 
 
-def pack_kernel(vel_ref, nu_ref, rows_ref, out_ref, turn_ref, table_ref):
+def pack_kernel(
+    vel_hbm, nu_hbm, rows_hbm, out_ref, table_ref, vel_ref, nu_ref, rows_ref, turn_ref, sems
+):
+    copies = [
+        pltpu.make_async_copy(vel_hbm, vel_ref, sems.at[0]),
+        pltpu.make_async_copy(nu_hbm, nu_ref, sems.at[1]),
+        pltpu.make_async_copy(rows_hbm, rows_ref, sems.at[2]),
+    ]
+    for copy in copies:
+        copy.start()
+    copies[0].wait()
     for f in range(4):
+        if f == 3:
+            copies[1].wait()
         block = vel_ref[f] if f < 3 else nu_ref[...]
         for half in range(2):
             turn_ref[half, pl.ds(f, CZ, stride=4), :] = block[half * 128:half * 128 + 128].T
@@ -64,6 +76,7 @@
         high, low = in_two(turn_ref[half])
         table_ref[:, half * 128:half * 128 + 128] = high
         table_ref[:, ROWS + half * 128:ROWS + half * 128 + 128] = low
+    copies[2].wait()
     top = lax.broadcasted_iota(i32, (8, 128), 0) < 4
 
     def step(pair, carry):
@@ -81,13 +94,10 @@
         out_ref[pl.ds(pl.multiple_of(pair * 8, 8), 8), :] = jnp.where(top, first, second)
         return carry
 
-    lax.fori_loop(0, rows_ref.shape[0] // 2, step, 0, unroll=4)
-
-
-def prepare_kernel(
-    tiles_ref, place_ref, pitch_ref, s0_ref, s1_ref, s2_ref, s3_ref, vel_ref, nu_ref, cell_ref,
-    base_ref, wall_ref, hot_ref, low_ref, depth_ref, span_ref
-):
+    lax.fori_loop(0, 32, step, 0, unroll=4)
+
+
+def prepare_kernel(vel_ref, nu_ref, cell_ref, base_ref, hot_ref, low_ref):
     for pair in range(8):
         cell = two_rows(cell_ref, pair)
         hot_ref[:, pair * 256:(pair + 1) * 256] = one_hot(cell >> 7, ROWS)
@@ -100,19 +110,23 @@
         block = vel_ref[f] if f < 3 else nu_ref[...]
         base_ref[f] = jnp.where(ghost, 0.0, block)
 
+
+def wall_kernel(
+    tiles_ref, pitch_ref, near_ref, far_ref, wall_ref, depth_ref, span_ref
+):
     angle = jnp.full((1, 128), pitch_ref[0], f32)
     cosine = jnp.cos(angle)
     sine = jnp.sin(angle)
     turned = []
-    for ref in (s0_ref, s1_ref, s2_ref, s3_ref):
-        x, y, z = ref[0:1, :], ref[1:2, :], ref[2:3, :]
+    for ref, n in ((near_ref, 0), (near_ref, 3), (far_ref, 0), (far_ref, 3)):
+        x, y, z = ref[n:n + 1, :], ref[n + 1:n + 2, :], ref[n + 2:n + 3, :]
         turned.append((cosine * x + sine * z, y, cosine * z - sine * x))
     depth = lax.broadcasted_iota(i32, (CZ, 128), 0).astype(f32) + (0.5 - 0.5 * CZ)
     for q in range(4):
         step_z = depth - turned[q][2]
         depth_ref[q] = step_z * step_z
     wall_ref[...] = jnp.full(wall_ref.shape, dist_cap, f32)
-    start = place_ref[1] * CY
+    start = lax.axis_index("gy") * CY
     for slot in range(8):
         tile = tiles_ref[slot]
 
@@ -139,7 +153,7 @@
 
 def fill_kernel(
     inc_ref, src_ref, weight_ref, cell_ref, base_ref,
-    filled_ref, xlo_ref, xhi_ref, ylo_ref, yhi_ref, zlo_ref, zhi_ref,
+    filled_ref, x1_ref, x2_ref, y1_ref, y2_ref, z1_ref, z2_ref,
     table_ref, hot_ref, value_ref, flat_ref
 ):
     high, low = in_two(inc_ref[...])
@@ -178,44 +192,54 @@
     added = lax.dot_general(
         hot_ref[...], value_ref[...], (((1,), (1,)), ((), ())), preferred_element_type=f32
     )
+    even_x, even_y, even_z = [(lax.axis_index(axis) & 1) == 0 for axis in ("gx", "gy", "gz")]
     for f in range(4):
         block = base_ref[f] + added[:, f * CZ:(f + 1) * CZ]
         filled_ref[f] = block
         flat_ref[pl.ds(f * ROWS, ROWS), :] = block
-        xlo_ref[pl.ds(f * 64, 64), :] = block[:64]
-        xhi_ref[pl.ds(f * 64, 64), :] = block[ROWS - 64:]
+        low, high = block[:64], block[ROWS - 64:]
+        x1_ref[pl.ds(f * 64, 64), :] = jnp.where(even_x, high, low)
+        x2_ref[pl.ds(f * 64, 64), :] = jnp.where(even_x, low, high)
     for h in range(2):
-        ylo_ref[pl.ds(h * 32, 32), :] = flat_ref[pl.ds(h, 32, stride=32), :]
-        yhi_ref[pl.ds(h * 32, 32), :] = flat_ref[pl.ds(30 + h, 32, stride=32), :]
+        low = flat_ref[pl.ds(h, 32, stride=32), :]
+        high = flat_ref[pl.ds(30 + h, 32, stride=32), :]
+        y1_ref[pl.ds(h * 32, 32), :] = jnp.where(even_y, high, low)
+        y2_ref[pl.ds(h * 32, 32), :] = jnp.where(even_y, low, high)
     for b in range(8):
         turn = flat_ref[pl.ds(b * 128, 128), :].T
-        zlo_ref[pl.ds(b * 2, 2), :] = turn[0:2]
-        zhi_ref[pl.ds(b * 2, 2), :] = turn[126:128]
+        z1_ref[pl.ds(b * 2, 2), :] = jnp.where(even_z, turn[126:128], turn[0:2])
+        z2_ref[pl.ds(b * 2, 2), :] = jnp.where(even_z, turn[0:2], turn[126:128])
 
 
 def advance_kernel(
-    place_ref, filled_ref, xlo_ref, xhi_ref, ylo_ref, yhi_ref, zlo_ref, zhi_ref, wall_ref, fluid_ref,
+    filled_ref, x1_ref, x2_ref, y1_ref, y2_ref, z1_ref, z2_ref, wall_ref, fluid_ref,
     vel_ref, nu_ref, pad_ref, edge_ref
 ):
-    ix, iy, iz = place_ref[0], place_ref[1], place_ref[2]
-    keep = lambda flag, value: jnp.where(flag, value, 0.0)
+    ix, iy, iz = lax.axis_index("gx"), lax.axis_index("gy"), lax.axis_index("gz")
+
+    def sides(index, last, first, second):
+        odd = (index & 1) == 1
+        below = jnp.where(odd, first, second)
+        above = jnp.where(odd, second, first)
+        return jnp.where(index > 0, below, 0.0), jnp.where(index < last, above, 0.0)
+
     for f in range(4):
         pad_ref[f, 2:10, 8:40, :] = filled_ref[f].reshape(8, 32, 128)
-        pad_ref[f, 0:2, 8:40, :] = keep(ix > 0, xlo_ref[f * 64:(f + 1) * 64, :]).reshape(2, 32, 128)
-        pad_ref[f, 10:12, 8:40, :] = keep(ix < 15, xhi_ref[f * 64:(f + 1) * 64, :]).reshape(2, 32, 128)
+        at = pl.ds(f * 64, 64)
+        below, above = sides(ix, 15, x1_ref[at, :], x2_ref[at, :])
+        pad_ref[f, 0:2, 8:40, :] = below.reshape(2, 32, 128)
+        pad_ref[f, 10:12, 8:40, :] = above.reshape(2, 32, 128)
+    below, above = sides(iy, 3, y1_ref[...], y2_ref[...])
     for h in range(2):
-        low = keep(iy > 0, ylo_ref[h * 32:(h + 1) * 32, :])
-        high = keep(iy < 3, yhi_ref[h * 32:(h + 1) * 32, :])
         for f in range(4):
             for i in range(8):
-                n = f * 8 + i
-                pad_ref[f, 2 + i, 6 + h:7 + h, :] = low[n:n + 1]
-                pad_ref[f, 2 + i, 40 + h:41 + h, :] = high[n:n + 1]
-    zlow = keep(iz > 0, zlo_ref[...])
-    zhigh = keep(iz < 3, zhi_ref[...])
+                n = h * 32 + f * 8 + i
+                pad_ref[f, 2 + i, 6 + h:7 + h, :] = below[n:n + 1]
+                pad_ref[f, 2 + i, 40 + h:41 + h, :] = above[n:n + 1]
+    below, above = sides(iz, 3, z1_ref[...], z2_ref[...])
     for b in range(8):
         block = jnp.concatenate(
-            [zhigh[2 * b:2 * b + 2], jnp.zeros((124, 128), f32), zlow[2 * b:2 * b + 2]], axis=0
+            [above[2 * b:2 * b + 2], jnp.zeros((124, 128), f32), below[2 * b:2 * b + 2]], axis=0
         )
         edge_ref[b // 2, (b % 2) * 4:(b % 2) * 4 + 4] = block.T.reshape(4, 32, 128)
 
@@ -279,11 +303,15 @@
     return pl.BlockSpec(memory_space=pltpu.VMEM)
 
 
+def anywhere():
+    return pl.BlockSpec(memory_space=pl.ANY)
+
+
 def smem():
     return pl.BlockSpec(memory_space=pltpu.SMEM)
 
 
-def call(kernel, out_shape, in_specs, scratch, name, flops, moved):
+def call(kernel, out_shape, in_specs, scratch, name, flops, moved, limit=VMEM_LIMIT):
     many = isinstance(out_shape, (list, tuple))
     return pl.pallas_call(
         kernel,
@@ -291,15 +319,26 @@
         in_specs=in_specs,
         out_specs=[vmem()] * len(out_shape) if many else vmem(),
         scratch_shapes=scratch,
-        compiler_params=pltpu.CompilerParams(vmem_limit_bytes=VMEM_LIMIT),
+        compiler_params=pltpu.CompilerParams(vmem_limit_bytes=limit),
         cost_estimate=pl.CostEstimate(flops=flops, bytes_accessed=moved, transcendentals=0),
         name=name,
     )
 
 
-def ring(block, axis, shift):
+def exchange(block, axis, bit):
     count = lax.axis_size(axis)
-    return lax.ppermute(block, axis, [(i, (i + shift) % count) for i in range(count)])
+    return lax.ppermute(block, axis, [(i, i ^ bit) for i in range(count)])
+
+
+def swap_up(block, axis):
+    return exchange(block, axis, 1)
+
+
+def swap_down(block, axis):
+    count = lax.axis_size(axis)
+    return lax.ppermute(
+        block, axis, [(i, (i + (1 if i % 2 else -1)) % count) for i in range(count)]
+    )
 
 
 def on_device(
@@ -310,28 +349,37 @@
     vel = velocity.reshape(3, ROWS, CZ)
     nu = nu_tilde.reshape(ROWS, CZ)
     cells = ghost_cell.reshape(16, 128)
-    place = jnp.stack([lax.axis_index("gx"), lax.axis_index("gy"), lax.axis_index("gz")]).astype(i32)
-    own = surface.reshape(3, 128)
-    others = [ring(own, "gy", d) for d in (1, 2, 3)]
+    rows = send_rows.reshape(64, 128)
+    points = surface.reshape(3, 128)
+    points = jnp.concatenate([points, exchange(points, "gy", 1)])
 
     outgoing = call(
-        pack_kernel, shape(256, 128), [vmem()] * 3,
-        [pltpu.VMEM((2, 512, 128), f32), pltpu.VMEM((512, 2 * ROWS), bf16)],
-        "pack_rows", 4_000_000_000, 1_000_000,
-    )(vel, nu, send_rows.reshape(64, 128))
+        pack_kernel, shape(256, 128), [anywhere()] * 3,
+        [pltpu.VMEM((512, 2 * ROWS), bf16),
+         pltpu.VMEM((3, ROWS, CZ), f32), pltpu.VMEM((ROWS, CZ), f32), pltpu.VMEM((64, 128), i32),
+         pltpu.VMEM((2, 512, 128), f32), pltpu.SemaphoreType.DMA((3,))],
+        "pack_rows", 4_000_000_000, 1_000_000, 60 * 1024 * 1024,
+    )(vel, nu, rows)
+    outgoing, points = lax.optimization_barrier((outgoing, points))
     incoming = lax.all_to_all(
         outgoing.reshape(256 * 128), ("gx", "gz"), split_axis=0, concat_axis=0, tiled=True
     ).reshape(256, 128)
-
-    base, wall = call(
-        prepare_kernel, (shape(4, ROWS, CZ), shape(32, TY, CZ)),
-        [smem()] * 3 + [vmem()] * 7,
-        [pltpu.VMEM((ROWS, 2048), bf16), pltpu.VMEM((CZ, 2048), bf16),
-         pltpu.VMEM((4, CZ, 128), f32), pltpu.VMEM((4, 8, 128), f32)],
+    far_points = exchange(points, "gy", 2)
+
+    base = call(
+        prepare_kernel, shape(4, ROWS, CZ), [vmem()] * 3,
+        [pltpu.VMEM((ROWS, 2048), bf16), pltpu.VMEM((CZ, 2048), bf16)],
         "prepare", 200_000_000, 2_000_000,
-    )(near_tiles.reshape(8), place, pitch_angle, own, *others, vel, nu, cells)
-
-    filled, xlo, xhi, ylo, yhi, zlo, zhi = call(
+    )(vel, nu, cells)
+
+    wall = call(
+        wall_kernel, shape(32, TY, CZ), [smem()] * 2 + [vmem()] * 2,
+        [pltpu.VMEM((4, CZ, 128), f32), pltpu.VMEM((4, 8, 128), f32)],
+        "wall", 30_000_000, 200_000,
+    )(near_tiles.reshape(8), pitch_angle, points, far_points)
+
+    base, wall = lax.optimization_barrier((base, wall))
+    filled, x1, x2, y1, y2, z1, z2 = call(
         fill_kernel,
         (shape(4, ROWS, CZ), shape(256, 128), shape(256, 128), shape(64, 128), shape(64, 128),
          shape(16, 128), shape(16, 128)),
@@ -341,16 +389,18 @@
         "fill_ghosts", 4_000_000_000, 2_000_000,
     )(incoming, ghost_src.reshape(8, 2048), ghost_weight.reshape(8, 2048), cells, base)
 
-    from_below = [ring(xhi, "gx", 1), ring(yhi, "gy", 1), ring(zhi, "gz", 1)]
-    from_above = [ring(xlo, "gx", -1), ring(ylo, "gy", -1), ring(zlo, "gz", -1)]
+    x1, x2 = swap_up(x1, "gx"), swap_down(x2, "gx")
+    y1, y2 = swap_up(y1, "gy"), swap_down(y2, "gy")
+    z1 = swap_up(z1, "gz")
+    z2, x1 = lax.optimization_barrier((z2, x1))
+    z2 = swap_down(z2, "gz")
+
     wall = wall.reshape(CX, CY, CZ)
     new_velocity, new_nu = call(
-        advance_kernel, (shape(3, CX, CY, CZ), shape(CX, CY, CZ)),
-        [smem()] + [vmem()] * 9,
+        advance_kernel, (shape(3, CX, CY, CZ), shape(CX, CY, CZ)), [vmem()] * 9,
         [pltpu.VMEM((4, 12, 48, CZ), f32), pltpu.VMEM((4, CX, CY, CZ), f32)],
         "advance", 20_000_000, 3_000_000,
-    )(place, filled, from_below[0], from_above[0], from_below[1], from_above[1],
-      from_below[2], from_above[2], wall, fluid_cells)
+    )(filled, x1, x2, y1, y2, z1, z2, wall, fluid_cells)
     return new_velocity, new_nu, wall
 
 

time: 59.4 us -> 53.1 us (0.89)
  the two profiles are of different devices: /device:TPU:6 before, /device:TPU:32 now
where the time goes in v2:
time: 53.1 us; the launch traced here: 52.9 us
  starting transfers between devices  23 us (43%)
  Pallas kernels  20 us (38%)
  waiting for transfers between devices  7.74 us (15%)
  between operations  1.38 us (3%)
  local copies, waits for them, and re-layouts  0.72 us (1%)
    all_to_all x1, starting transfers between devices, on_device(): lax.all_to_all(outgoing.reshape(256 * 128), ('gx', 'gz'), split_axis=0, c...  11.7 us
    pallas_call x1, Pallas kernels, on_device(): call(pack_kernel, shape(256, 128), [anywhere()] * 3, [pltpu.VMEM((512, 2...  8.12 us
    pallas_call x1, Pallas kernels, on_device(): call(fill_kernel, (shape(4, ROWS, CZ), shape(256, 128), shape(256, 128),...  6.85 us
    ppermute x3, starting transfers between devices, swap_down(): lax.ppermute(block, axis, [(i, (i + (1 if i % 2 else -1)) % count) for i...  5.67 us
    ppermute x5, starting transfers between devices, exchange(): return lax.ppermute(block, axis, [(i, i ^ bit) for i in range(count)])  5.64 us
    all_to_all x1, waiting for transfers between devices, on_device(): lax.all_to_all(outgoing.reshape(256 * 128), ('gx', 'gz'), split_axis=0, c...  3.07 us
    ppermute x5, waiting for transfers between devices, exchange(): return lax.ppermute(block, axis, [(i, i ^ bit) for i in range(count)])  2.93 us
    pallas_call x1, Pallas kernels, on_device(): call(advance_kernel, (shape(3, CX, CY, CZ), shape(CX, CY, CZ)), [vmem()]...  2.33 us
  transfers between devices with their start and end apart: 9, of which 4 were waited for; matrix products, arithmetic and copies ran while one was open for 0% of the time, Pallas kernels for 20%

profile of v2, /device:TPU:32, one launch (start us, length us, event | category | flops | bytes accessed | tf_op | source)
XLA Modules:
  0.0 52.9 jit_solution(5369762194982478605)
XLA Ops:
  0.6 0.7 %copy.16 = f32[1,1,3,128]{3,2,1,0:T(4,128)S(1)} copy(f32[1,1,3,128]{3,1,2,0:T(1,128)} %param.13) | data formatting | bytes 3072
  1.3 1.6 %collective-permute-start = (f32[3,128]{1,0:T(4,128)S(1)}, f32[3,128]{1,0:T(4,128)S(1)}, u32[]{:S(2)}, u32[]{:S(2)}) collective-permute-start(f32[3,128]{1,0:T(4,128)S(1)} %bitcast.26), channel_id=1, source_target_pairs={{0,4},{4,0},{8,12},{12,8},{1,5},{5,1},{9,13},{13,9},{2,6},{6,2},{1... | collective-permute-start | bytes 4616 | tf_op jit(solution)/shard_map/ppermute | solution.py:330
  2.9 8.1 %pack_rows.1 = f32[256,128]{1,0:T(8,128)} custom-call(f32[3,256,128]{2,1,0:T(8,128)} %bitcast.15, f32[256,128]{1,0:T(8,128)} %bitcast.18, s32[64,128]{1,0:T(8,128)} %bitcast.28), custom_call_target="tpu_custom_call" | custom-call | flops 4000000000 | bytes 1000000 | tf_op jit(solution)/shard_map/pack_rows/pallas_call | solution.py:356
  11.0 0.0 collective-permute-done
  11.1 0.0 copy-start.3
  11.1 0.0 copy-start.4
  11.1 11.7 %all-to-all-start = ((f32[64,512,1]{1,2,0:T(1,128)}), f32[64,512,1]{1,2,0:T(1,128)S(1)}, u32[]{:S(2)}, u32[]{:S(2)}) async-start(f32[64,512,1]{1,2,0:T(1,128)} %bitcast.25), calls=%async_computation | async-start | bytes 262144 | tf_op jit(solution)/shard_map/all_to_all | solution.py:364
  22.8 3.0 %collective-permute-start.1 = (f32[6,128]{1,0:T(8,128)S(1)}, f32[6,128]{1,0:T(8,128)S(1)}, u32[]{:S(2)}, u32[]{:S(2)}) collective-permute-start(f32[6,128]{1,0:T(8,128)S(1)} %pad_maximum_fusion.near_ref), channel_id=1, source_target_pairs={{0,8},{4,12},{8,0},{12,4},{1,9},{5,13},{9,1},{13,5},{2,10},{6,14},... | collective-permute-start | bytes 9224 | tf_op jit(solution)/shard_map/ppermute | solution.py:330
  25.8 0.4 prepare.1.base_ref
  26.9 0.0 copy-start.5
  26.9 1.1 %collective-permute-done.1.far_ref = f32[6,128]{1,0:T(8,128)S(1)} collective-permute-done((f32[6,128]{1,0:T(8,128)S(1)}, f32[6,128]{1,0:T(8,128)S(1)}, u32[]{:S(2)}, u32[]{:S(2)}) %collective-permute-start.1) | collective-permute-done | bytes 3104 | tf_op jit(solution)/shard_map/ppermute | solution.py:330
  28.0 2.3 %wall.1 = f32[32,8,128]{2,1,0:T(8,128)} custom-call(s32[8]{0:T(128)S(1)} %bitcast.22, f32[1]{0:T(128)S(6)} %copy.17.pitch_ref, f32[6,128]{1,0:T(8,128)S(1)} %pad_maximum_fusion.near_ref, f32[6,128]{1,0:T(8,128)S(1)} %collective-permute-done.1.far_ref), custom_call_target="tpu_custom_call" | custom-call | flops 30000000 | bytes 200000 | tf_op jit(solution)/shard_map/wall/pallas_call | solution.py:375
  30.3 3.1 %all-to-all-done = f32[64,512,1]{1,2,0:T(1,128)S(1)} async-done(((f32[64,512,1]{1,2,0:T(1,128)}), f32[64,512,1]{1,2,0:T(1,128)S(1)}, u32[]{:S(2)}, u32[]{:S(2)}) %all-to-all-start) | async-done | bytes 131104 | tf_op jit(solution)/shard_map/all_to_all | solution.py:364
  33.4 6.8 %fill_ghosts.1 = (f32[4,256,128]{2,1,0:T(8,128)S(1)}, f32[256,128]{1,0:T(8,128)S(1)}, f32[256,128]{1,0:T(8,128)S(1)}, f32[64,128]{1,0:T(8,128)S(1)}, f32[64,128]...) custom-call(f32[256,128]{1,0:T(8,128)S(1)} %bitcast.17, s32[8,2048]{1,0:T(8,128)S(1)} %bitcast.23, ...), custom_call_target="tpu_custom_call" | custom-call | flops 4000000000 | bytes 2000000 | tf_op jit(solution)/shard_map/fill_ghosts/pallas_call | solution.py:382
  40.2 0.1 collective-permute-start.2
  40.3 1.4 %collective-permute-start.3 = (f32[256,128]{1,0:T(8,128)S(1)}, f32[256,128]{1,0:T(8,128)S(1)}, u32[]{:S(2)}, u32[]{:S(2)}) collective-permute-start(f32[256,128]{1,0:T(8,128)S(1)} %get-tuple-element.25), channel_id=1, source_target_pairs={{0,240},{16,32},{32,16},{48,64},{64,48},{80,96},{96,80},{112,128},... | collective-permute-start | bytes 393224 | tf_op jit(solution)/shard_map/ppermute | solution.py:339
  41.7 0.4 collective-permute-start.4
  42.1 3.0 %collective-permute-start.5 = (f32[64,128]{1,0:T(8,128)S(1)}, f32[64,128]{1,0:T(8,128)S(1)}, u32[]{:S(2)}, u32[]{:S(2)}) collective-permute-start(f32[64,128]{1,0:T(8,128)S(1)} %get-tuple-element.27), channel_id=1, source_target_pairs={{0,12},{4,8},{8,4},{12,0},{1,13},{5,9},{9,5},{13,1},{2,14},{6,10},... | collective-permute-start | bytes 98312 | tf_op jit(solution)/shard_map/ppermute | solution.py:339
  45.2 0.5 %collective-permute-start.6 = (f32[16,128]{1,0:T(8,128)S(1)}, f32[16,128]{1,0:T(8,128)S(1)}, u32[]{:S(2)}, u32[]{:S(2)}) collective-permute-start(f32[16,128]{1,0:T(8,128)S(1)} %get-tuple-element.28), channel_id=1, source_target_pairs={{0,1},{1,0},{2,3},{3,2},{4,5},{5,4},{6,7},{7,6},{8,9},{9,8},{10,11... | collective-permute-start | bytes 24584 | tf_op jit(solution)/shard_map/ppermute | solution.py:330
  45.7 1.3 %collective-permute-start.7 = (f32[16,128]{1,0:T(8,128)S(1)}, f32[16,128]{1,0:T(8,128)S(1)}, u32[]{:S(2)}, u32[]{:S(2)}) collective-permute-start(f32[16,128]{1,0:T(8,128)S(1)} %get-tuple-element.29), channel_id=1, source_target_pairs={{0,3},{1,2},{2,1},{3,0},{4,7},{5,6},{6,5},{7,4},{8,11},{9,10},{10,... | collective-permute-start | bytes 24584 | tf_op jit(solution)/shard_map/ppermute | solution.py:339
  47.0 1.8 %collective-permute-done.6.z1_ref = f32[16,128]{1,0:T(8,128)S(1)} collective-permute-done((f32[16,128]{1,0:T(8,128)S(1)}, f32[16,128]{1,0:T(8,128)S(1)}, u32[]{:S(2)}, u32[]{:S(2)}) %collective-permute-start.6) | collective-permute-done | bytes 8224 | tf_op jit(solution)/shard_map/ppermute | solution.py:330
  48.8 0.0 collective-permute-done.4.y1_ref
  48.8 1.7 %collective-permute-done.7.z2_ref = f32[16,128]{1,0:T(8,128)S(1)} collective-permute-done((f32[16,128]{1,0:T(8,128)S(1)}, f32[16,128]{1,0:T(8,128)S(1)}, u32[]{:S(2)}, u32[]{:S(2)}) %collective-permute-start.7) | collective-permute-done | bytes 8224 | tf_op jit(solution)/shard_map/ppermute | solution.py:339
  50.6 2.3 %advance.1 = (f32[3,8,32,128]{3,2,1,0:T(8,128)}, f32[8,32,128]{2,1,0:T(8,128)}) custom-call(f32[4,256,128]{2,1,0:T(8,128)S(1)} %get-tuple-element.21.filled_ref, f32[256,128]{1,0:T(8,128)S(1)} %collective-permute-done.2.x1_ref, f32[256,128]{1,0:T(8,128)S(1)} %collective-permute-done.3.x2_ref, f32[64,128]{1,0:T(8,128)S(1)} %collective-permute-done.4.y1_ref, ...), custom_call_target="tpu_custom_call" | custom-call | flops 20000000 | bytes 3000000 | tf_op jit(solution)/shard_map/advance/pallas_call | solution.py:399
  (17 shorter events, 0.0 us)
Async XLA Ops:
  1.3 9.7 %collective-permute-start = (f32[3,128]{1,0:T(4,128)S(1)}, f32[3,128]{1,0:T(4,128)S(1)}, u32[]{:S(2)}, u32[]{:S(2)}) collective-permute-start(f32[3,128]{1,0:T(4,128)S(1)} %bitcast.26), channel_id=1, source_target_pairs={{0,4},{4,0},{8,12},{12,8},{1,5},{5,1},{9,13},{13,9},{2,6},{6,2},{1... | collective-permute-start | bytes 4616 | tf_op jit(solution)/shard_map/ppermute | solution.py:330
  2.9 22.9 %copy-start.1 = (f32[3,8,32,128]{3,2,1,0:T(8,128)S(1)}, f32[3,8,32,128]{3,2,1,0:T(8,128)}, u32[]{:S(2)}) copy-start(f32[3,8,32,128]{3,2,1,0:T(8,128)} %param.10) | copy-start | bytes 1179652
  11.1 14.8 %copy-start.3 = (f32[8,32,128]{2,1,0:T(8,128)S(1)}, f32[8,32,128]{2,1,0:T(8,128)}, u32[]{:S(2)}) copy-start(f32[8,32,128]{2,1,0:T(8,128)} %param.11) | copy-start | bytes 393220
  11.1 14.8 %copy-start.4 = (s32[1,1,1,2048]{3,2,1,0:T(1,128)S(1)}, s32[1,1,1,2048]{3,2,1,0:T(1,128)}, u32[]{:S(2)}) copy-start(s32[1,1,1,2048]{3,2,1,0:T(1,128)} %param.17) | copy-start | bytes 24580
  11.1 22.3 %all-to-all-start = ((f32[64,512,1]{1,2,0:T(1,128)}), f32[64,512,1]{1,2,0:T(1,128)S(1)}, u32[]{:S(2)}, u32[]{:S(2)}) async-start(f32[64,512,1]{1,2,0:T(1,128)} %bitcast.25), calls=%async_computation | async-start | bytes 262144 | tf_op jit(solution)/shard_map/all_to_all | solution.py:364
  22.8 5.2 %collective-permute-start.1 = (f32[6,128]{1,0:T(8,128)S(1)}, f32[6,128]{1,0:T(8,128)S(1)}, u32[]{:S(2)}, u32[]{:S(2)}) collective-permute-start(f32[6,128]{1,0:T(8,128)S(1)} %pad_maximum_fusion.near_ref), channel_id=1, source_target_pairs={{0,8},{4,12},{8,0},{12,4},{1,9},{5,13},{9,1},{13,5},{2,10},{6,14},... | collective-permute-start | bytes 9224 | tf_op jit(solution)/shard_map/ppermute | solution.py:330
  26.9 1.1 %copy-start.5 = (s32[1,1,1,8]{3,2,1,0:T(1,128)S(1)}, s32[1,1,1,8]{3,2,1,0:T(1,128)}, u32[]{:S(2)}) copy-start(s32[1,1,1,8]{3,2,1,0:T(1,128)} %param.15) | copy-start | bytes 100
  28.0 5.3 %copy-start.6 = (s32[1,1,1,8,2048]{4,3,2,1,0:T(8,128)S(1)}, s32[1,1,1,8,2048]{4,3,2,1,0:T(8,128)}, u32[]{:S(2)}) copy-start(s32[1,1,1,8,2048]{4,3,2,1,0:T(8,128)} %param.18) | copy-start | bytes 196612
  28.0 5.3 %copy-start.7 = (f32[1,1,1,8,2048]{4,3,2,1,0:T(8,128)S(1)}, f32[1,1,1,8,2048]{4,3,2,1,0:T(8,128)}, u32[]{:S(2)}) copy-start(f32[1,1,1,8,2048]{4,3,2,1,0:T(8,128)} %param.19) | copy-start | bytes 196612
  33.4 17.2 %copy-start = (f32[32,8,128]{2,1,0:T(8,128)S(1)}, f32[32,8,128]{2,1,0:T(8,128)}, u32[]{:S(2)}) copy-start(f32[32,8,128]{2,1,0:T(8,128)} %wall.1) | copy-start | bytes 393220
  33.4 17.2 %copy-start.2 = (s32[8,32,128]{2,1,0:T(8,128)S(1)}, s32[8,32,128]{2,1,0:T(8,128)}, u32[]{:S(2)}) copy-start(s32[8,32,128]{2,1,0:T(8,128)} %fluid_ref.1) | copy-start | bytes 393220
  40.2 5.5 %collective-permute-start.2 = (f32[256,128]{1,0:T(8,128)S(1)}, f32[256,128]{1,0:T(8,128)S(1)}, u32[]{:S(2)}, u32[]{:S(2)}) collective-permute-start(f32[256,128]{1,0:T(8,128)S(1)} %get-tuple-element.23), channel_id=1, source_target_pairs={{0,16},{16,0},{32,48},{48,32},{64,80},{80,64},{96,112},{112,96},{1... | collective-permute-start | bytes 393224 | tf_op jit(solution)/shard_map/ppermute | solution.py:330
  40.3 8.5 %collective-permute-start.3 = (f32[256,128]{1,0:T(8,128)S(1)}, f32[256,128]{1,0:T(8,128)S(1)}, u32[]{:S(2)}, u32[]{:S(2)}) collective-permute-start(f32[256,128]{1,0:T(8,128)S(1)} %get-tuple-element.25), channel_id=1, source_target_pairs={{0,240},{16,32},{32,16},{48,64},{64,48},{80,96},{96,80},{112,128},... | collective-permute-start | bytes 393224 | tf_op jit(solution)/shard_map/ppermute | solution.py:339
  41.7 7.1 %collective-permute-start.4 = (f32[64,128]{1,0:T(8,128)S(1)}, f32[64,128]{1,0:T(8,128)S(1)}, u32[]{:S(2)}, u32[]{:S(2)}) collective-permute-start(f32[64,128]{1,0:T(8,128)S(1)} %get-tuple-element.26), channel_id=1, source_target_pairs={{0,4},{4,0},{8,12},{12,8},{1,5},{5,1},{9,13},{13,9},{2,6},{6,2},{1... | collective-permute-start | bytes 98312 | tf_op jit(solution)/shard_map/ppermute | solution.py:330
  42.1 6.7 %collective-permute-start.5 = (f32[64,128]{1,0:T(8,128)S(1)}, f32[64,128]{1,0:T(8,128)S(1)}, u32[]{:S(2)}, u32[]{:S(2)}) collective-permute-start(f32[64,128]{1,0:T(8,128)S(1)} %get-tuple-element.27), channel_id=1, source_target_pairs={{0,12},{4,8},{8,4},{12,0},{1,13},{5,9},{9,5},{13,1},{2,14},{6,10},... | collective-permute-start | bytes 98312 | tf_op jit(solution)/shard_map/ppermute | solution.py:339
  45.2 3.7 %collective-permute-start.6 = (f32[16,128]{1,0:T(8,128)S(1)}, f32[16,128]{1,0:T(8,128)S(1)}, u32[]{:S(2)}, u32[]{:S(2)}) collective-permute-start(f32[16,128]{1,0:T(8,128)S(1)} %get-tuple-element.28), channel_id=1, source_target_pairs={{0,1},{1,0},{2,3},{3,2},{4,5},{5,4},{6,7},{7,6},{8,9},{9,8},{10,11... | collective-permute-start | bytes 24584 | tf_op jit(solution)/shard_map/ppermute | solution.py:330
  45.7 4.9 %collective-permute-start.7 = (f32[16,128]{1,0:T(8,128)S(1)}, f32[16,128]{1,0:T(8,128)S(1)}, u32[]{:S(2)}, u32[]{:S(2)}) collective-permute-start(f32[16,128]{1,0:T(8,128)S(1)} %get-tuple-element.29), channel_id=1, source_target_pairs={{0,3},{1,2},{2,1},{3,0},{4,7},{5,6},{6,5},{7,4},{8,11},{9,10},{10,... | collective-permute-start | bytes 24584 | tf_op jit(solution)/shard_map/ppermute | solution.py:339

commit v3 on v2

--- a/solution.py
+++ b/solution.py
@@ -26,7 +26,7 @@
 dist_cap = 8.0
 time_step = 0.05
 
-VMEM_LIMIT = 48 * 1024 * 1024
+VMEM_LIMIT = 24 * 1024 * 1024
 
 
 def in_two(values):
@@ -35,8 +35,8 @@
 
 
 def one_hot(index, count):
-    level = lax.broadcasted_iota(i32, (count, index.shape[1]), 0)
-    return jnp.where(level == index, 1.0, 0.0).astype(bf16)
+    level = lax.broadcasted_iota(i32, (count, 1), 0).astype(f32).astype(bf16)
+    return jnp.where(level == index.astype(f32).astype(bf16), jnp.ones((), bf16), jnp.zeros((), bf16))
 
 
 def pick_group(values, index):
@@ -94,7 +94,7 @@
         out_ref[pl.ds(pl.multiple_of(pair * 8, 8), 8), :] = jnp.where(top, first, second)
         return carry
 
-    lax.fori_loop(0, 32, step, 0, unroll=4)
+    lax.fori_loop(0, 32, step, 0, unroll=32)
 
 
 def prepare_kernel(vel_ref, nu_ref, cell_ref, base_ref, hot_ref, low_ref):
@@ -111,50 +111,61 @@
         base_ref[f] = jnp.where(ghost, 0.0, block)
 
 
-def wall_kernel(
-    tiles_ref, pitch_ref, near_ref, far_ref, wall_ref, depth_ref, span_ref
-):
-    angle = jnp.full((1, 128), pitch_ref[0], f32)
+def turn_points(pitch_ref, near_ref, far_ref, depth_ref):
+    angle = jnp.broadcast_to(pitch_ref[...], (1, 128))
     cosine = jnp.cos(angle)
     sine = jnp.sin(angle)
+    depth = lax.broadcasted_iota(i32, (CZ, 128), 0).astype(f32) + (0.5 - 0.5 * CZ)
     turned = []
-    for ref, n in ((near_ref, 0), (near_ref, 3), (far_ref, 0), (far_ref, 3)):
-        x, y, z = ref[n:n + 1, :], ref[n + 1:n + 2, :], ref[n + 2:n + 3, :]
-        turned.append((cosine * x + sine * z, y, cosine * z - sine * x))
-    depth = lax.broadcasted_iota(i32, (CZ, 128), 0).astype(f32) + (0.5 - 0.5 * CZ)
+    for q, (ref, n) in enumerate(((near_ref, 0), (near_ref, 3), (far_ref, 0), (far_ref, 3))):
+        x, y, z = ref[n], ref[n + 1], ref[n + 2]
+        turned.append((cosine * x + sine * z, y))
+        step_z = depth - (cosine * z - sine * x)
+        depth_ref[q] = step_z * step_z
+    return turned
+
+
+def tile_at(tiles_ref, slot):
+    return jnp.max(tiles_ref[:, slot:slot + 1].astype(f32)).astype(i32)
+
+
+def tile_distance(tile, turned, depth_ref, span_ref):
+    coord_x = (tile // 4).astype(f32) + (0.5 - 0.5 * CX)
+    first = (tile % 4) * TY + lax.axis_index("gy") * CY
+    coord_y = (lax.broadcasted_iota(i32, (8, 128), 0) + first).astype(f32) + (0.5 - 0.5 * 4 * CY)
     for q in range(4):
-        step_z = depth - turned[q][2]
-        depth_ref[q] = step_z * step_z
+        step_x = coord_x - turned[q][0]
+        step_y = coord_y - turned[q][1]
+        span_ref[q] = step_x * step_x + step_y * step_y
+    rows = []
+    for r in range(8):
+        least = None
+        for q in range(4):
+            here = span_ref[q, r:r + 1, :] + depth_ref[q]
+            least = here if least is None else jnp.minimum(least, here)
+        rows.append(jnp.min(least.T, axis=0, keepdims=True))
+    return jnp.minimum(jnp.sqrt(jnp.concatenate(rows, axis=0) + dist_eps), dist_cap)
+
+
+def wall_kernel(
+    tiles_ref, pitch_ref, near_ref, far_ref, wall_ref, again_ref, depth_ref, span_ref
+):
+    tiles = [tile_at(tiles_ref, slot) for slot in range(8)]
+    turned = turn_points(pitch_ref, near_ref, far_ref, depth_ref)
     wall_ref[...] = jnp.full(wall_ref.shape, dist_cap, f32)
-    start = lax.axis_index("gy") * CY
     for slot in range(8):
-        tile = tiles_ref[slot]
-
-        @pl.when(tile >= 0)
+
+        @pl.when(tiles[slot] >= 0)
         def _():
-            coord_x = (tile // 4).astype(f32) + (0.5 - 0.5 * CX)
-            first = (tile % 4) * TY + start
-            row = lax.broadcasted_iota(i32, (8, 128), 0) + first
-            coord_y = row.astype(f32) + (0.5 - 0.5 * 4 * CY)
-            for q in range(4):
-                step_x = coord_x - turned[q][0]
-                step_y = coord_y - turned[q][1]
-                span_ref[q] = step_x * step_x + step_y * step_y
-            rows = []
-            for r in range(8):
-                least = None
-                for q in range(4):
-                    here = span_ref[q, r:r + 1, :] + depth_ref[q]
-                    least = here if least is None else jnp.minimum(least, here)
-                rows.append(jnp.min(least.T, axis=0, keepdims=True))
-            nearest = jnp.concatenate(rows, axis=0)
-            wall_ref[tile] = jnp.minimum(jnp.sqrt(nearest + dist_eps), dist_cap)
+            wall_ref[tiles[slot]] = tile_distance(tiles[slot], turned, depth_ref, span_ref)
+
+    again_ref[...] = wall_ref[...]
 
 
 def fill_kernel(
-    inc_ref, src_ref, weight_ref, cell_ref, base_ref,
+    inc_ref, src_ref, weight_ref, base_ref, hot_ref, low_ref,
     filled_ref, x1_ref, x2_ref, y1_ref, y2_ref, z1_ref, z2_ref,
-    table_ref, hot_ref, value_ref, flat_ref
+    table_ref, value_ref, flat_ref
 ):
     high, low = in_two(inc_ref[...])
     table_ref[:, :CZ] = high
@@ -174,24 +185,19 @@
             value = jnp.where((peer & 1) == 1, both[4:], both[:4])
             total = total + weight_ref[t:t + 1, at] * value
         total = -total
-        cell = two_rows(cell_ref, block)
-        hot = one_hot(cell >> 7, ROWS)
-        put = pl.multiple_of(block * 512, 512)
-        hot_ref[:, pl.ds(put, 256)] = hot
-        hot_ref[:, pl.ds(put + 256, 256)] = hot
-        here = lax.broadcasted_iota(i32, (CZ, 256), 0) == (cell & 127)
-        rest = total - total.astype(bf16).astype(f32)
+        high = total.astype(bf16).astype(f32)
+        rest = total - high
+        low_hot = low_ref[:, at]
         for f in range(4):
-            value_ref[pl.ds(f * CZ, CZ), pl.ds(put, 256)] = jnp.where(
-                here, total[f:f + 1], 0.0).astype(bf16)
-            value_ref[pl.ds(f * CZ, CZ), pl.ds(put + 256, 256)] = jnp.where(
-                here, rest[f:f + 1], 0.0).astype(bf16)
+            value_ref[pl.ds(f * CZ, CZ), at] = low_hot * high[f:f + 1].astype(bf16)
+            value_ref[pl.ds((4 + f) * CZ, CZ), at] = low_hot * rest[f:f + 1].astype(bf16)
         return carry
 
-    lax.fori_loop(0, 8, step, 0)
+    lax.fori_loop(0, 8, step, 0, unroll=8)
     added = lax.dot_general(
         hot_ref[...], value_ref[...], (((1,), (1,)), ((), ())), preferred_element_type=f32
     )
+    added = added[:, :4 * CZ] + added[:, 4 * CZ:]
     even_x, even_y, even_z = [(lax.axis_index(axis) & 1) == 0 for axis in ("gx", "gy", "gz")]
     for f in range(4):
         block = base_ref[f] + added[:, f * CZ:(f + 1) * CZ]
@@ -296,7 +302,7 @@
             nu_ref[i, 8 * c:8 * c + 8, :] = working + mask * nu_rhs
         return carry
 
-    lax.fori_loop(0, 8, plane, 0)
+    lax.fori_loop(0, 8, plane, 0, unroll=8)
 
 
 def vmem():
@@ -305,10 +311,6 @@
 
 def anywhere():
     return pl.BlockSpec(memory_space=pl.ANY)
-
-
-def smem():
-    return pl.BlockSpec(memory_space=pltpu.SMEM)
 
 
 def call(kernel, out_shape, in_specs, scratch, name, flops, moved, limit=VMEM_LIMIT):
@@ -350,9 +352,6 @@
     nu = nu_tilde.reshape(ROWS, CZ)
     cells = ghost_cell.reshape(16, 128)
     rows = send_rows.reshape(64, 128)
-    points = surface.reshape(3, 128)
-    points = jnp.concatenate([points, exchange(points, "gy", 1)])
-
     outgoing = call(
         pack_kernel, shape(256, 128), [anywhere()] * 3,
         [pltpu.VMEM((512, 2 * ROWS), bf16),
@@ -360,34 +359,35 @@
          pltpu.VMEM((2, 512, 128), f32), pltpu.SemaphoreType.DMA((3,))],
         "pack_rows", 4_000_000_000, 1_000_000, 60 * 1024 * 1024,
     )(vel, nu, rows)
-    outgoing, points = lax.optimization_barrier((outgoing, points))
+    points, outgoing = lax.optimization_barrier((surface.reshape(3, 1, 128), outgoing))
     incoming = lax.all_to_all(
         outgoing.reshape(256 * 128), ("gx", "gz"), split_axis=0, concat_axis=0, tiled=True
     ).reshape(256, 128)
+    points = jnp.concatenate([points, exchange(points, "gy", 1)])
     far_points = exchange(points, "gy", 2)
 
-    base = call(
-        prepare_kernel, shape(4, ROWS, CZ), [vmem()] * 3,
-        [pltpu.VMEM((ROWS, 2048), bf16), pltpu.VMEM((CZ, 2048), bf16)],
-        "prepare", 200_000_000, 2_000_000,
+    base, hot, low_hot = call(
+        prepare_kernel,
+        (shape(4, ROWS, CZ), shape(ROWS, 2048, dtype=bf16), shape(CZ, 2048, dtype=bf16)),
+        [vmem()] * 3, [], "prepare", 200_000_000, 2_000_000,
     )(vel, nu, cells)
-
-    wall = call(
-        wall_kernel, shape(32, TY, CZ), [smem()] * 2 + [vmem()] * 2,
-        [pltpu.VMEM((4, CZ, 128), f32), pltpu.VMEM((4, 8, 128), f32)],
-        "wall", 30_000_000, 200_000,
-    )(near_tiles.reshape(8), pitch_angle, points, far_points)
-
-    base, wall = lax.optimization_barrier((base, wall))
+    points, base = lax.optimization_barrier((points, base))
+
     filled, x1, x2, y1, y2, z1, z2 = call(
         fill_kernel,
         (shape(4, ROWS, CZ), shape(256, 128), shape(256, 128), shape(64, 128), shape(64, 128),
          shape(16, 128), shape(16, 128)),
-        [vmem()] * 5,
-        [pltpu.VMEM((256, 256), bf16), pltpu.VMEM((ROWS, 4096), bf16),
-         pltpu.VMEM((512, 4096), bf16), pltpu.VMEM((4 * ROWS, CZ), f32)],
+        [vmem()] * 6,
+        [pltpu.VMEM((256, 256), bf16), pltpu.VMEM((1024, 2048), bf16),
+         pltpu.VMEM((4 * ROWS, CZ), f32)],
         "fill_ghosts", 4_000_000_000, 2_000_000,
-    )(incoming, ghost_src.reshape(8, 2048), ghost_weight.reshape(8, 2048), cells, base)
+    )(incoming, ghost_src.reshape(8, 2048), ghost_weight.reshape(8, 2048), base, hot, low_hot)
+
+    far_points, x1 = lax.optimization_barrier((far_points, x1))
+    wall, wall_again = call(
+        wall_kernel, (shape(32, TY, CZ), shape(32, TY, CZ)), [vmem()] * 4,
+        [pltpu.VMEM((4, CZ, 128), f32), pltpu.VMEM((4, 8, 128), f32)], "wall", 30_000_000, 200_000,
+    )(near_tiles.reshape(1, 8), pitch_angle.reshape(1, 1), points, far_points)
 
     x1, x2 = swap_up(x1, "gx"), swap_down(x2, "gx")
     y1, y2 = swap_up(y1, "gy"), swap_down(y2, "gy")
@@ -400,7 +400,7 @@
         advance_kernel, (shape(3, CX, CY, CZ), shape(CX, CY, CZ)), [vmem()] * 9,
         [pltpu.VMEM((4, 12, 48, CZ), f32), pltpu.VMEM((4, CX, CY, CZ), f32)],
         "advance", 20_000_000, 3_000_000,
-    )(filled, x1, x2, y1, y2, z1, z2, wall, fluid_cells)
+    )(filled, x1, x2, y1, y2, z1, z2, wall_again.reshape(CX, CY, CZ), fluid_cells)
     return new_velocity, new_nu, wall
 
 

time: 53.1 us -> 46.2 us (0.87)
  Pallas kernels: 20 us -> 15.2 us
  waiting for transfers between devices: 7.74 us -> 5.5 us
  local copies, waits for them, and re-layouts: 0.72 us -> 0.05 us
  starting transfers between devices: 23 us -> 23.6 us
    pallas_call x1, Pallas kernels: 6.85 us -> 3.68 us  [on_device(): call(fill_kernel, (shape(4, ROWS, CZ), shape(256, 128), shape(256, 128),...]
    pallas_call x1, Pallas kernels: 8.12 us -> 6.62 us  [on_device(): call(pack_kernel, shape(256, 128), [anywhere()] * 3, [pltpu.VMEM((512, 2...]
    ppermute x5, waiting for transfers between devices: 2.93 us -> 1.5 us  [exchange(): return lax.ppermute(block, axis, [(i, i ^ bit) for i in range(count)])]
    ppermute x5, starting transfers between devices: 5.64 us -> 7.06 us  [exchange(): return lax.ppermute(block, axis, [(i, i ^ bit) for i in range(count)])]
    ppermute x3, waiting for transfers between devices: 1.74 us -> 0.34 us  [swap_down(): lax.ppermute(block, axis, [(i, (i + (1 if i % 2 else -1)) % count) for i...]
    ppermute x3, starting transfers between devices: 5.67 us -> 4.85 us  [swap_down(): lax.ppermute(block, axis, [(i, (i + (1 if i % 2 else -1)) % count) for i...]
    unnamed x17, local copies, waits for them, and re-layouts: 0.72 us -> 0.05 us
    all_to_all x1, waiting for transfers between devices: 3.07 us -> 3.66 us  [on_device(): lax.all_to_all(outgoing.reshape(256 * 128), ('gx', 'gz'), split_axis=0, c...]
  transfers between devices with their start and end apart: 9 -> 9, of which waited for: 4 -> 3; matrix products, arithmetic and copies ran while one was open for 0% -> 0% of each run, Pallas kernels for 20% -> 15%
where the time goes in v3:
time: 46.2 us; the launch traced here: 45.8 us
  starting transfers between devices  23.6 us (51%)
  Pallas kernels  15.2 us (33%)
  waiting for transfers between devices  5.5 us (12%)
  between operations  1.43 us (3%)
    all_to_all x1, starting transfers between devices, on_device(): lax.all_to_all(outgoing.reshape(256 * 128), ('gx', 'gz'), split_axis=0, c...  11.7 us
    ppermute x5, starting transfers between devices, exchange(): return lax.ppermute(block, axis, [(i, i ^ bit) for i in range(count)])  7.06 us
    pallas_call x1, Pallas kernels, on_device(): call(pack_kernel, shape(256, 128), [anywhere()] * 3, [pltpu.VMEM((512, 2...  6.62 us
    ppermute x3, starting transfers between devices, swap_down(): lax.ppermute(block, axis, [(i, (i + (1 if i % 2 else -1)) % count) for i...  4.85 us
    pallas_call x1, Pallas kernels, on_device(): call(fill_kernel, (shape(4, ROWS, CZ), shape(256, 128), shape(256, 128),...  3.68 us
    all_to_all x1, waiting for transfers between devices, on_device(): lax.all_to_all(outgoing.reshape(256 * 128), ('gx', 'gz'), split_axis=0, c...  3.66 us
    pallas_call x1, Pallas kernels, on_device(): call(wall_kernel, (shape(32, TY, CZ), shape(32, TY, CZ)), [vmem()] * 4, [...  2.55 us
    pallas_call x1, Pallas kernels, on_device(): call(advance_kernel, (shape(3, CX, CY, CZ), shape(CX, CY, CZ)), [vmem()]...  1.88 us
  transfers between devices with their start and end apart: 9, of which 3 were waited for; matrix products, arithmetic and copies ran while one was open for 0% of the time, Pallas kernels for 15%

profile of v3, /device:TPU:32, one launch (start us, length us, event | category | flops | bytes accessed | tf_op | source)
XLA Modules:
  0.0 45.8 jit_solution(2980430701426986924)
XLA Ops:
  0.6 6.6 %pack_rows.1 = f32[256,128]{1,0:T(8,128)} custom-call(f32[3,256,128]{2,1,0:T(8,128)} %bitcast.16, f32[256,128]{1,0:T(8,128)} %bitcast.18, s32[64,128]{1,0:T(8,128)} %bitcast.27), custom_call_target="tpu_custom_call" | custom-call | flops 4000000000 | bytes 1000000 | tf_op jit(solution)/shard_map/pack_rows/pallas_call | solution.py:355
  7.3 0.0 copy-start.7
  7.3 0.0 copy-start.2
  7.3 0.0 copy-start.5
  7.3 11.7 %all-to-all-start = ((f32[64,512,1]{1,2,0:T(1,128)}), f32[64,512,1]{1,2,0:T(1,128)S(1)}, u32[]{:S(2)}, u32[]{:S(2)}) async-start(f32[64,512,1]{1,2,0:T(1,128)} %bitcast.24), calls=%async_computation | async-start | bytes 262144 | tf_op jit(solution)/shard_map/all_to_all | solution.py:363
  19.1 1.7 %collective-permute-start = (f32[3,1,128]{2,1,0:T(1,128)S(1)}, f32[3,1,128]{2,1,0:T(1,128)S(1)}, u32[]{:S(2)}, u32[]{:S(2)}) collective-permute-start(f32[3,1,128]{2,1,0:T(1,128)S(1)} %bitcast.25), channel_id=1, source_target_pairs={{0,4},{4,0},{8,12},{12,8},{1,5},{5,1},{9,13},{13,9},{2,6},{6,2},{1... | collective-permute-start | bytes 4616 | tf_op jit(solution)/shard_map/ppermute | solution.py:332
  20.7 0.0 copy-start.3
  20.7 0.0 copy-start.4
  20.8 0.5 %prepare.1 = (f32[4,256,128]{2,1,0:T(8,128)S(1)}, bf16[256,2048]{1,0:T(8,128)(2,1)S(1)}, bf16[128,2048]{1,0:T(8,128)(2,1)S(1)}) custom-call(f32[3,256,128]{2,1,0:T(8,128)S(1)} %bitcast.17, f32[256,128]{1,0:T(8,128)S(1)} %bitcast.19, s32[16,128]{1,0:T(8,128)S(1)} %bitcast.22), custom_call_target="tpu_custom_call" | custom-call | flops 200000000 | bytes 2000000 | tf_op jit(solution)/shard_map/prepare/pallas_call | solution.py:369
  21.2 1.5 %collective-permute-done = f32[3,1,128]{2,1,0:T(1,128)S(1)} collective-permute-done((f32[3,1,128]{2,1,0:T(1,128)S(1)}, f32[3,1,128]{2,1,0:T(1,128)S(1)}, u32[]{:S(2)}, u32[]{:S(2)}) %collective-permute-start) | collective-permute-done | bytes 1568 | tf_op jit(solution)/shard_map/ppermute | solution.py:332
  22.7 3.2 %collective-permute-start.1 = (f32[6,1,128]{2,1,0:T(1,128)S(1)}, f32[6,1,128]{2,1,0:T(1,128)S(1)}, u32[]{:S(2)}, u32[]{:S(2)}) collective-permute-start(f32[6,1,128]{2,1,0:T(1,128)S(1)} %constant_dynamic-update-slice_fusion.near_ref), channel_id=1, source_target_pairs={{0,8},{4,12},{8,0},{12,4},{1,9},{5,13},{9,1},{13,5},{2,10},{6,14},... | collective-permute-start | bytes 9224 | tf_op jit(solution)/shard_map/ppermute | solution.py:332
  25.9 3.7 %all-to-all-done = f32[64,512,1]{1,2,0:T(1,128)S(1)} async-done(((f32[64,512,1]{1,2,0:T(1,128)}), f32[64,512,1]{1,2,0:T(1,128)S(1)}, u32[]{:S(2)}, u32[]{:S(2)}) %all-to-all-start) | async-done | bytes 131104 | tf_op jit(solution)/shard_map/all_to_all | solution.py:363
  29.6 3.7 %fill_ghosts.1 = (f32[4,256,128]{2,1,0:T(8,128)S(1)}, f32[256,128]{1,0:T(8,128)S(1)}, f32[256,128]{1,0:T(8,128)S(1)}, f32[64,128]{1,0:T(8,128)S(1)}, f32[64,128]...) custom-call(f32[256,128]{1,0:T(8,128)S(1)} %bitcast.15, s32[8,2048]{1,0:T(8,128)S(1)} %bitcast.20, ...), custom_call_target="tpu_custom_call" | custom-call | flops 4000000000 | bytes 2000000 | tf_op jit(solution)/shard_map/fill_ghosts/pallas_call | solution.py:376
  33.3 0.0 copy-start
  33.3 0.0 collective-permute-done.1.far_ref
  33.3 0.1 collective-permute-start.2
  33.4 1.4 %collective-permute-start.3 = (f32[256,128]{1,0:T(8,128)S(1)}, f32[256,128]{1,0:T(8,128)S(1)}, u32[]{:S(2)}, u32[]{:S(2)}) collective-permute-start(f32[256,128]{1,0:T(8,128)S(1)} %get-tuple-element.36), channel_id=1, source_target_pairs={{0,240},{16,32},{32,16},{48,64},{64,48},{80,96},{96,80},{112,128},... | collective-permute-start | bytes 393224 | tf_op jit(solution)/shard_map/ppermute | solution.py:341
  34.8 1.6 %collective-permute-start.4 = (f32[64,128]{1,0:T(8,128)S(1)}, f32[64,128]{1,0:T(8,128)S(1)}, u32[]{:S(2)}, u32[]{:S(2)}) collective-permute-start(f32[64,128]{1,0:T(8,128)S(1)} %get-tuple-element.37), channel_id=1, source_target_pairs={{0,4},{4,0},{8,12},{12,8},{1,5},{5,1},{9,13},{13,9},{2,6},{6,2},{1... | collective-permute-start | bytes 98312 | tf_op jit(solution)/shard_map/ppermute | solution.py:332
  36.4 2.2 %collective-permute-start.5 = (f32[64,128]{1,0:T(8,128)S(1)}, f32[64,128]{1,0:T(8,128)S(1)}, u32[]{:S(2)}, u32[]{:S(2)}) collective-permute-start(f32[64,128]{1,0:T(8,128)S(1)} %get-tuple-element.38), channel_id=1, source_target_pairs={{0,12},{4,8},{8,4},{12,0},{1,13},{5,9},{9,5},{13,1},{2,14},{6,10},... | collective-permute-start | bytes 98312 | tf_op jit(solution)/shard_map/ppermute | solution.py:341
  38.5 0.5 %collective-permute-start.6 = (f32[16,128]{1,0:T(8,128)S(1)}, f32[16,128]{1,0:T(8,128)S(1)}, u32[]{:S(2)}, u32[]{:S(2)}) collective-permute-start(f32[16,128]{1,0:T(8,128)S(1)} %get-tuple-element.39), channel_id=1, source_target_pairs={{0,1},{1,0},{2,3},{3,2},{4,5},{5,4},{6,7},{7,6},{8,9},{9,8},{10,11... | collective-permute-start | bytes 24584 | tf_op jit(solution)/shard_map/ppermute | solution.py:332
  39.1 1.3 %collective-permute-start.7 = (f32[16,128]{1,0:T(8,128)S(1)}, f32[16,128]{1,0:T(8,128)S(1)}, u32[]{:S(2)}, u32[]{:S(2)}) collective-permute-start(f32[16,128]{1,0:T(8,128)S(1)} %get-tuple-element.40), channel_id=1, source_target_pairs={{0,3},{1,2},{2,1},{3,0},{4,7},{5,6},{6,5},{7,4},{8,11},{9,10},{10,... | collective-permute-start | bytes 24584 | tf_op jit(solution)/shard_map/ppermute | solution.py:341
  41.0 2.6 %wall.1 = (f32[32,8,128]{2,1,0:T(8,128)}, f32[32,8,128]{2,1,0:T(8,128)S(1)}) custom-call(s32[1,8]{1,0:T(1,128)S(1)} %bitcast.23, f32[1,1]{1,0:T(1,128)} %bitcast.13.pitch_ref, f32[6,1,128]{2,1,0:T(1,128)S(1)} %constant_dynamic-update-slice_fusion.near_ref, f32[6,1,128]{2,1,0:T(1,128)S(1)} %collective-permute-done.1.far_ref), custom_call_target="tpu_custom_call" | custom-call | flops 30000000 | bytes 200000 | tf_op jit(solution)/shard_map/wall/pallas_call | solution.py:387
  43.6 0.3 collective-permute-done.7.z2_ref
  43.9 1.9 %advance.1 = (f32[3,8,32,128]{3,2,1,0:T(8,128)}, f32[8,32,128]{2,1,0:T(8,128)}) custom-call(f32[4,256,128]{2,1,0:T(8,128)S(1)} %get-tuple-element.31.filled_ref, f32[256,128]{1,0:T(8,128)S(1)} %collective-permute-done.2.x1_ref, f32[256,128]{1,0:T(8,128)S(1)} %collective-permute-done.3.x2_ref, f32[64,128]{1,0:T(8,128)S(1)} %collective-permute-done.4.y1_ref, ...), custom_call_target="tpu_custom_call" | custom-call | flops 20000000 | bytes 3000000 | tf_op jit(solution)/shard_map/advance/pallas_call | solution.py:399
  (17 shorter events, 0.0 us)
Async XLA Ops:
  0.6 20.1 %copy-start.1 = (f32[3,8,32,128]{3,2,1,0:T(8,128)S(1)}, f32[3,8,32,128]{3,2,1,0:T(8,128)}, u32[]{:S(2)}) copy-start(f32[3,8,32,128]{3,2,1,0:T(8,128)} %param.10) | copy-start | bytes 1179652
  7.3 11.8 %copy-start.7 = (f32[1,1,3,128]{3,1,2,0:T(1,128)S(1)}, f32[1,1,3,128]{3,1,2,0:T(1,128)}, u32[]{:S(2)}) copy-start(f32[1,1,3,128]{3,1,2,0:T(1,128)} %param.13) | copy-start | bytes 4612
  7.3 13.4 %copy-start.2 = (f32[8,32,128]{2,1,0:T(8,128)S(1)}, f32[8,32,128]{2,1,0:T(8,128)}, u32[]{:S(2)}) copy-start(f32[8,32,128]{2,1,0:T(8,128)} %param.11) | copy-start | bytes 393220
  7.3 13.4 %copy-start.5 = (s32[1,1,1,2048]{3,2,1,0:T(1,128)S(1)}, s32[1,1,1,2048]{3,2,1,0:T(1,128)}, u32[]{:S(2)}) copy-start(s32[1,1,1,2048]{3,2,1,0:T(1,128)} %param.17) | copy-start | bytes 24580
  7.3 22.3 %all-to-all-start = ((f32[64,512,1]{1,2,0:T(1,128)}), f32[64,512,1]{1,2,0:T(1,128)S(1)}, u32[]{:S(2)}, u32[]{:S(2)}) async-start(f32[64,512,1]{1,2,0:T(1,128)} %bitcast.24), calls=%async_computation | async-start | bytes 262144 | tf_op jit(solution)/shard_map/all_to_all | solution.py:363
  19.1 3.7 %collective-permute-start = (f32[3,1,128]{2,1,0:T(1,128)S(1)}, f32[3,1,128]{2,1,0:T(1,128)S(1)}, u32[]{:S(2)}, u32[]{:S(2)}) collective-permute-start(f32[3,1,128]{2,1,0:T(1,128)S(1)} %bitcast.25), channel_id=1, source_target_pairs={{0,4},{4,0},{8,12},{12,8},{1,5},{5,1},{9,13},{13,9},{2,6},{6,2},{1... | collective-permute-start | bytes 4616 | tf_op jit(solution)/shard_map/ppermute | solution.py:332
  20.7 8.9 %copy-start.3 = (s32[1,1,1,8,2048]{4,3,2,1,0:T(8,128)S(1)}, s32[1,1,1,8,2048]{4,3,2,1,0:T(8,128)}, u32[]{:S(2)}) copy-start(s32[1,1,1,8,2048]{4,3,2,1,0:T(8,128)} %param.18) | copy-start | bytes 196612
  20.7 8.8 %copy-start.4 = (f32[1,1,1,8,2048]{4,3,2,1,0:T(8,128)S(1)}, f32[1,1,1,8,2048]{4,3,2,1,0:T(8,128)}, u32[]{:S(2)}) copy-start(f32[1,1,1,8,2048]{4,3,2,1,0:T(8,128)} %param.19) | copy-start | bytes 196612
  22.7 10.6 %collective-permute-start.1 = (f32[6,1,128]{2,1,0:T(1,128)S(1)}, f32[6,1,128]{2,1,0:T(1,128)S(1)}, u32[]{:S(2)}, u32[]{:S(2)}) collective-permute-start(f32[6,1,128]{2,1,0:T(1,128)S(1)} %constant_dynamic-update-slice_fusion.near_ref), channel_id=1, source_target_pairs={{0,8},{4,12},{8,0},{12,4},{1,9},{5,13},{9,1},{13,5},{2,10},{6,14},... | collective-permute-start | bytes 9224 | tf_op jit(solution)/shard_map/ppermute | solution.py:332
  29.6 11.4 %copy-start.6 = (s32[1,1,1,8]{3,2,1,0:T(1,128)S(1)}, s32[1,1,1,8]{3,2,1,0:T(1,128)}, u32[]{:S(2)}) copy-start(s32[1,1,1,8]{3,2,1,0:T(1,128)} %param.15) | copy-start | bytes 100
  33.3 10.7 %copy-start = (s32[8,32,128]{2,1,0:T(8,128)S(1)}, s32[8,32,128]{2,1,0:T(8,128)}, u32[]{:S(2)}) copy-start(s32[8,32,128]{2,1,0:T(8,128)} %fluid_ref.1) | copy-start | bytes 393220
  33.3 5.8 %collective-permute-start.2 = (f32[256,128]{1,0:T(8,128)S(1)}, f32[256,128]{1,0:T(8,128)S(1)}, u32[]{:S(2)}, u32[]{:S(2)}) collective-permute-start(f32[256,128]{1,0:T(8,128)S(1)} %get-tuple-element.34), channel_id=1, source_target_pairs={{0,16},{16,0},{32,48},{48,32},{64,80},{80,64},{96,112},{112,96},{1... | collective-permute-start | bytes 393224 | tf_op jit(solution)/shard_map/ppermute | solution.py:332
  33.4 10.2 %collective-permute-start.3 = (f32[256,128]{1,0:T(8,128)S(1)}, f32[256,128]{1,0:T(8,128)S(1)}, u32[]{:S(2)}, u32[]{:S(2)}) collective-permute-start(f32[256,128]{1,0:T(8,128)S(1)} %get-tuple-element.36), channel_id=1, source_target_pairs={{0,240},{16,32},{32,16},{48,64},{64,48},{80,96},{96,80},{112,128},... | collective-permute-start | bytes 393224 | tf_op jit(solution)/shard_map/ppermute | solution.py:341
  34.8 8.8 %collective-permute-start.4 = (f32[64,128]{1,0:T(8,128)S(1)}, f32[64,128]{1,0:T(8,128)S(1)}, u32[]{:S(2)}, u32[]{:S(2)}) collective-permute-start(f32[64,128]{1,0:T(8,128)S(1)} %get-tuple-element.37), channel_id=1, source_target_pairs={{0,4},{4,0},{8,12},{12,8},{1,5},{5,1},{9,13},{13,9},{2,6},{6,2},{1... | collective-permute-start | bytes 98312 | tf_op jit(solution)/shard_map/ppermute | solution.py:332
  36.4 7.2 %collective-permute-start.5 = (f32[64,128]{1,0:T(8,128)S(1)}, f32[64,128]{1,0:T(8,128)S(1)}, u32[]{:S(2)}, u32[]{:S(2)}) collective-permute-start(f32[64,128]{1,0:T(8,128)S(1)} %get-tuple-element.38), channel_id=1, source_target_pairs={{0,12},{4,8},{8,4},{12,0},{1,13},{5,9},{9,5},{13,1},{2,14},{6,10},... | collective-permute-start | bytes 98312 | tf_op jit(solution)/shard_map/ppermute | solution.py:341
  38.5 5.0 %collective-permute-start.6 = (f32[16,128]{1,0:T(8,128)S(1)}, f32[16,128]{1,0:T(8,128)S(1)}, u32[]{:S(2)}, u32[]{:S(2)}) collective-permute-start(f32[16,128]{1,0:T(8,128)S(1)} %get-tuple-element.39), channel_id=1, source_target_pairs={{0,1},{1,0},{2,3},{3,2},{4,5},{5,4},{6,7},{7,6},{8,9},{9,8},{10,11... | collective-permute-start | bytes 24584 | tf_op jit(solution)/shard_map/ppermute | solution.py:332
  39.1 4.9 %collective-permute-start.7 = (f32[16,128]{1,0:T(8,128)S(1)}, f32[16,128]{1,0:T(8,128)S(1)}, u32[]{:S(2)}, u32[]{:S(2)}) collective-permute-start(f32[16,128]{1,0:T(8,128)S(1)} %get-tuple-element.40), channel_id=1, source_target_pairs={{0,3},{1,2},{2,1},{3,0},{4,7},{5,6},{6,5},{7,4},{8,11},{9,10},{10,... | collective-permute-start | bytes 24584 | tf_op jit(solution)/shard_map/ppermute | solution.py:341

commit v4 on v3

--- a/solution.py
+++ b/solution.py
@@ -97,7 +97,10 @@
     lax.fori_loop(0, 32, step, 0, unroll=32)
 
 
-def prepare_kernel(vel_ref, nu_ref, cell_ref, base_ref, hot_ref, low_ref):
+def prepare_kernel(vel_ref, nu_ref, cell_ref, pitch_ref, base_ref, hot_ref, low_ref, trig_ref):
+    angle = jnp.broadcast_to(pitch_ref[...], (1, 128))
+    trig_ref[0:1, :] = jnp.cos(angle)
+    trig_ref[1:2, :] = jnp.sin(angle)
     for pair in range(8):
         cell = two_rows(cell_ref, pair)
         hot_ref[:, pair * 256:(pair + 1) * 256] = one_hot(cell >> 7, ROWS)
@@ -111,10 +114,8 @@
         base_ref[f] = jnp.where(ghost, 0.0, block)
 
 
-def turn_points(pitch_ref, near_ref, far_ref, depth_ref):
-    angle = jnp.broadcast_to(pitch_ref[...], (1, 128))
-    cosine = jnp.cos(angle)
-    sine = jnp.sin(angle)
+def turn_points(trig_ref, near_ref, far_ref, depth_ref):
+    cosine, sine = trig_ref[0:1, :], trig_ref[1:2, :]
     depth = lax.broadcasted_iota(i32, (CZ, 128), 0).astype(f32) + (0.5 - 0.5 * CZ)
     turned = []
     for q, (ref, n) in enumerate(((near_ref, 0), (near_ref, 3), (far_ref, 0), (far_ref, 3))):
@@ -148,10 +149,10 @@
 
 
 def wall_kernel(
-    tiles_ref, pitch_ref, near_ref, far_ref, wall_ref, again_ref, depth_ref, span_ref
+    tiles_ref, trig_ref, near_ref, far_ref, wall_ref, again_ref, depth_ref, span_ref
 ):
     tiles = [tile_at(tiles_ref, slot) for slot in range(8)]
-    turned = turn_points(pitch_ref, near_ref, far_ref, depth_ref)
+    turned = turn_points(trig_ref, near_ref, far_ref, depth_ref)
     wall_ref[...] = jnp.full(wall_ref.shape, dist_cap, f32)
     for slot in range(8):
 
@@ -366,11 +367,12 @@
     points = jnp.concatenate([points, exchange(points, "gy", 1)])
     far_points = exchange(points, "gy", 2)
 
-    base, hot, low_hot = call(
+    base, hot, low_hot, trig = call(
         prepare_kernel,
-        (shape(4, ROWS, CZ), shape(ROWS, 2048, dtype=bf16), shape(CZ, 2048, dtype=bf16)),
-        [vmem()] * 3, [], "prepare", 200_000_000, 2_000_000,
-    )(vel, nu, cells)
+        (shape(4, ROWS, CZ), shape(ROWS, 2048, dtype=bf16), shape(CZ, 2048, dtype=bf16),
+         shape(2, 128)),
+        [vmem()] * 4, [], "prepare", 200_000_000, 2_000_000,
+    )(vel, nu, cells, pitch_angle.reshape(1, 1))
     points, base = lax.optimization_barrier((points, base))
 
     filled, x1, x2, y1, y2, z1, z2 = call(
@@ -387,7 +389,7 @@
     wall, wall_again = call(
         wall_kernel, (shape(32, TY, CZ), shape(32, TY, CZ)), [vmem()] * 4,
         [pltpu.VMEM((4, CZ, 128), f32), pltpu.VMEM((4, 8, 128), f32)], "wall", 30_000_000, 200_000,
-    )(near_tiles.reshape(1, 8), pitch_angle.reshape(1, 1), points, far_points)
+    )(near_tiles.reshape(1, 8), trig, points, far_points)
 
     x1, x2 = swap_up(x1, "gx"), swap_down(x2, "gx")
     y1, y2 = swap_up(y1, "gy"), swap_down(y2, "gy")

time: 46.2 us -> 46 us (level)
  Pallas kernels: 15.2 us -> 14.4 us
  waiting for transfers between devices: 5.5 us -> 6.25 us
    ppermute x3, waiting for transfers between devices: 0.34 us -> 1.74 us  [swap_down(): lax.ppermute(block, axis, [(i, (i + (1 if i % 2 else -1)) % count) for i...]
    pallas_call x1, Pallas kernels: 2.55 us -> 1.78 us  [on_device(): call(wall_kernel, (shape(32, TY, CZ), shape(32, TY, CZ)), [vmem()] * 4, [...]
    ppermute x5, waiting for transfers between devices: 1.5 us -> 0.85 us  [exchange(): return lax.ppermute(block, axis, [(i, i ^ bit) for i in range(count)])]
  transfers between devices with their start and end apart: 9 -> 9, of which waited for: 3 -> 3; matrix products, arithmetic and copies ran while one was open for 0% -> 0% of each run, Pallas kernels for 15% -> 13%
where the time goes in v4:
time: 46 us; the launch traced here: 45.8 us
  starting transfers between devices  23.6 us (51%)
  Pallas kernels  14.4 us (31%)
  waiting for transfers between devices  6.25 us (14%)
  between operations  1.44 us (3%)
    all_to_all x1, starting transfers between devices, on_device(): lax.all_to_all(outgoing.reshape(256 * 128), ('gx', 'gz'), split_axis=0, c...  11.7 us
    ppermute x5, starting transfers between devices, exchange(): return lax.ppermute(block, axis, [(i, i ^ bit) for i in range(count)])  7.06 us
    pallas_call x1, Pallas kernels, on_device(): call(pack_kernel, shape(256, 128), [anywhere()] * 3, [pltpu.VMEM((512, 2...  6.62 us
    ppermute x3, starting transfers between devices, swap_down(): lax.ppermute(block, axis, [(i, (i + (1 if i % 2 else -1)) % count) for i...  4.85 us
    pallas_call x1, Pallas kernels, on_device(): call(fill_kernel, (shape(4, ROWS, CZ), shape(256, 128), shape(256, 128),...  3.68 us
    all_to_all x1, waiting for transfers between devices, on_device(): lax.all_to_all(outgoing.reshape(256 * 128), ('gx', 'gz'), split_axis=0, c...  3.65 us
    pallas_call x1, Pallas kernels, on_device(): call(advance_kernel, (shape(3, CX, CY, CZ), shape(CX, CY, CZ)), [vmem()]...  1.87 us
    pallas_call x1, Pallas kernels, on_device(): call(wall_kernel, (shape(32, TY, CZ), shape(32, TY, CZ)), [vmem()] * 4, [...  1.78 us
  transfers between devices with their start and end apart: 9, of which 3 were waited for; matrix products, arithmetic and copies ran while one was open for 0% of the time, Pallas kernels for 13%

profile of v4, /device:TPU:32, one launch (start us, length us, event | category | flops | bytes accessed | tf_op | source)
XLA Modules:
  0.0 45.8 jit_solution(2084610519010534811)
XLA Ops:
  0.6 6.6 %pack_rows.1 = f32[256,128]{1,0:T(8,128)} custom-call(f32[3,256,128]{2,1,0:T(8,128)} %bitcast.16, f32[256,128]{1,0:T(8,128)} %bitcast.18, s32[64,128]{1,0:T(8,128)} %bitcast.27), custom_call_target="tpu_custom_call" | custom-call | flops 4000000000 | bytes 1000000 | tf_op jit(solution)/shard_map/pack_rows/pallas_call | solution.py:356
  7.3 0.0 copy-start.7
  7.3 0.0 copy-start.2
  7.3 11.7 %all-to-all-start = ((f32[64,512,1]{1,2,0:T(1,128)}), f32[64,512,1]{1,2,0:T(1,128)S(1)}, u32[]{:S(2)}, u32[]{:S(2)}) async-start(f32[64,512,1]{1,2,0:T(1,128)} %bitcast.24), calls=%async_computation | async-start | bytes 262144 | tf_op jit(solution)/shard_map/all_to_all | solution.py:364
  19.0 0.0 copy-start.5
  19.1 1.7 %collective-permute-start = (f32[3,1,128]{2,1,0:T(1,128)S(1)}, f32[3,1,128]{2,1,0:T(1,128)S(1)}, u32[]{:S(2)}, u32[]{:S(2)}) collective-permute-start(f32[3,1,128]{2,1,0:T(1,128)S(1)} %bitcast.25), channel_id=1, source_target_pairs={{0,4},{4,0},{8,12},{12,8},{1,5},{5,1},{9,13},{13,9},{2,6},{6,2},{1... | collective-permute-start | bytes 4616 | tf_op jit(solution)/shard_map/ppermute | solution.py:333
  21.4 0.0 copy-start.3
  21.4 0.0 copy-start.4
  21.4 0.5 %prepare.1 = (f32[4,256,128]{2,1,0:T(8,128)S(1)}, bf16[256,2048]{1,0:T(8,128)(2,1)S(1)}, bf16[128,2048]{1,0:T(8,128)(2,1)S(1)}, f32[2,128]{1,0:T(2,128)S(1)}) custom-call(f32[3,256,128]{2,1,0:T(8,128)S(1)} %bitcast.17, f32[256,128]{1,0:T(8,128)S(1)} %bitcast.19, s32[16,128]{1,0:T(8,128)S(1)} %bitcast.22, f32[1,1]{1,0:T(1,128)} %bitcast.13.pitch_ref), custom_call_target="tpu_custom_call" | custom-call | flops 200000000 | bytes 2000000 | tf_op jit(solution)/shard_map/prepare/pallas_call | solution.py:370
  21.9 0.8 %collective-permute-done = f32[3,1,128]{2,1,0:T(1,128)S(1)} collective-permute-done((f32[3,1,128]{2,1,0:T(1,128)S(1)}, f32[3,1,128]{2,1,0:T(1,128)S(1)}, u32[]{:S(2)}, u32[]{:S(2)}) %collective-permute-start) | collective-permute-done | bytes 1568 | tf_op jit(solution)/shard_map/ppermute | solution.py:333
  22.7 3.2 %collective-permute-start.1 = (f32[6,1,128]{2,1,0:T(1,128)S(1)}, f32[6,1,128]{2,1,0:T(1,128)S(1)}, u32[]{:S(2)}, u32[]{:S(2)}) collective-permute-start(f32[6,1,128]{2,1,0:T(1,128)S(1)} %constant_dynamic-update-slice_fusion.near_ref), channel_id=1, source_target_pairs={{0,8},{4,12},{8,0},{12,4},{1,9},{5,13},{9,1},{13,5},{2,10},{6,14},... | collective-permute-start | bytes 9224 | tf_op jit(solution)/shard_map/ppermute | solution.py:333
  25.9 3.7 %all-to-all-done = f32[64,512,1]{1,2,0:T(1,128)S(1)} async-done(((f32[64,512,1]{1,2,0:T(1,128)}), f32[64,512,1]{1,2,0:T(1,128)S(1)}, u32[]{:S(2)}, u32[]{:S(2)}) %all-to-all-start) | async-done | bytes 131104 | tf_op jit(solution)/shard_map/all_to_all | solution.py:364
  29.6 3.7 %fill_ghosts.1 = (f32[4,256,128]{2,1,0:T(8,128)S(1)}, f32[256,128]{1,0:T(8,128)S(1)}, f32[256,128]{1,0:T(8,128)S(1)}, f32[64,128]{1,0:T(8,128)S(1)}, f32[64,128]...) custom-call(f32[256,128]{1,0:T(8,128)S(1)} %bitcast.15, s32[8,2048]{1,0:T(8,128)S(1)} %bitcast.20, ...), custom_call_target="tpu_custom_call" | custom-call | flops 4000000000 | bytes 2000000 | tf_op jit(solution)/shard_map/fill_ghosts/pallas_call | solution.py:378
  33.3 0.0 copy-start
  33.3 0.1 collective-permute-start.2
  33.4 1.4 %collective-permute-start.3 = (f32[256,128]{1,0:T(8,128)S(1)}, f32[256,128]{1,0:T(8,128)S(1)}, u32[]{:S(2)}, u32[]{:S(2)}) collective-permute-start(f32[256,128]{1,0:T(8,128)S(1)} %get-tuple-element.37), channel_id=1, source_target_pairs={{0,240},{16,32},{32,16},{48,64},{64,48},{80,96},{96,80},{112,128},... | collective-permute-start | bytes 393224 | tf_op jit(solution)/shard_map/ppermute | solution.py:342
  34.8 1.6 %collective-permute-start.4 = (f32[64,128]{1,0:T(8,128)S(1)}, f32[64,128]{1,0:T(8,128)S(1)}, u32[]{:S(2)}, u32[]{:S(2)}) collective-permute-start(f32[64,128]{1,0:T(8,128)S(1)} %get-tuple-element.38), channel_id=1, source_target_pairs={{0,4},{4,0},{8,12},{12,8},{1,5},{5,1},{9,13},{13,9},{2,6},{6,2},{1... | collective-permute-start | bytes 98312 | tf_op jit(solution)/shard_map/ppermute | solution.py:333
  36.3 2.2 %collective-permute-start.5 = (f32[64,128]{1,0:T(8,128)S(1)}, f32[64,128]{1,0:T(8,128)S(1)}, u32[]{:S(2)}, u32[]{:S(2)}) collective-permute-start(f32[64,128]{1,0:T(8,128)S(1)} %get-tuple-element.39), channel_id=1, source_target_pairs={{0,12},{4,8},{8,4},{12,0},{1,13},{5,9},{9,5},{13,1},{2,14},{6,10},... | collective-permute-start | bytes 98312 | tf_op jit(solution)/shard_map/ppermute | solution.py:342
  38.5 0.5 %collective-permute-start.6 = (f32[16,128]{1,0:T(8,128)S(1)}, f32[16,128]{1,0:T(8,128)S(1)}, u32[]{:S(2)}, u32[]{:S(2)}) collective-permute-start(f32[16,128]{1,0:T(8,128)S(1)} %get-tuple-element.40), channel_id=1, source_target_pairs={{0,1},{1,0},{2,3},{3,2},{4,5},{5,4},{6,7},{7,6},{8,9},{9,8},{10,11... | collective-permute-start | bytes 24584 | tf_op jit(solution)/shard_map/ppermute | solution.py:333
  39.1 1.3 %collective-permute-start.7 = (f32[16,128]{1,0:T(8,128)S(1)}, f32[16,128]{1,0:T(8,128)S(1)}, u32[]{:S(2)}, u32[]{:S(2)}) collective-permute-start(f32[16,128]{1,0:T(8,128)S(1)} %get-tuple-element.41), channel_id=1, source_target_pairs={{0,3},{1,2},{2,1},{3,0},{4,7},{5,6},{6,5},{7,4},{8,11},{9,10},{10,... | collective-permute-start | bytes 24584 | tf_op jit(solution)/shard_map/ppermute | solution.py:342
  40.4 1.8 %wall.1 = (f32[32,8,128]{2,1,0:T(8,128)}, f32[32,8,128]{2,1,0:T(8,128)S(1)}) custom-call(s32[1,8]{1,0:T(1,128)S(1)} %bitcast.23, f32[2,128]{1,0:T(2,128)S(1)} %get-tuple-element.42.trig_ref, f32[6,1,128]{2,1,0:T(1,128)S(1)} %constant_dynamic-update-slice_fusion.near_ref, f32[6,1,128]{2,1,0:T(1,128)S(1)} %collective-permute-done.1.far_ref), custom_call_target="tpu_custom_call" | custom-call | flops 30000000 | bytes 200000 | tf_op jit(solution)/shard_map/wall/pallas_call | solution.py:389
  42.1 0.0 collective-permute-done.6.z1_ref
  42.2 1.7 %collective-permute-done.7.z2_ref = f32[16,128]{1,0:T(8,128)S(1)} collective-permute-done((f32[16,128]{1,0:T(8,128)S(1)}, f32[16,128]{1,0:T(8,128)S(1)}, u32[]{:S(2)}, u32[]{:S(2)}) %collective-permute-start.7) | collective-permute-done | bytes 8224 | tf_op jit(solution)/shard_map/ppermute | solution.py:342
  43.9 1.9 %advance.1 = (f32[3,8,32,128]{3,2,1,0:T(8,128)}, f32[8,32,128]{2,1,0:T(8,128)}) custom-call(f32[4,256,128]{2,1,0:T(8,128)S(1)} %get-tuple-element.32.filled_ref, f32[256,128]{1,0:T(8,128)S(1)} %collective-permute-done.2.x1_ref, f32[256,128]{1,0:T(8,128)S(1)} %collective-permute-done.3.x2_ref, f32[64,128]{1,0:T(8,128)S(1)} %collective-permute-done.4.y1_ref, ...), custom_call_target="tpu_custom_call" | custom-call | flops 20000000 | bytes 3000000 | tf_op jit(solution)/shard_map/advance/pallas_call | solution.py:401
  (17 shorter events, 0.0 us)
Async XLA Ops:
  0.6 20.8 %copy-start.1 = (f32[3,8,32,128]{3,2,1,0:T(8,128)S(1)}, f32[3,8,32,128]{3,2,1,0:T(8,128)}, u32[]{:S(2)}) copy-start(f32[3,8,32,128]{3,2,1,0:T(8,128)} %param.10) | copy-start | bytes 1179652
  7.3 11.8 %copy-start.7 = (f32[1,1,3,128]{3,1,2,0:T(1,128)S(1)}, f32[1,1,3,128]{3,1,2,0:T(1,128)}, u32[]{:S(2)}) copy-start(f32[1,1,3,128]{3,1,2,0:T(1,128)} %param.13) | copy-start | bytes 4612
  7.3 14.1 %copy-start.2 = (f32[8,32,128]{2,1,0:T(8,128)S(1)}, f32[8,32,128]{2,1,0:T(8,128)}, u32[]{:S(2)}) copy-start(f32[8,32,128]{2,1,0:T(8,128)} %param.11) | copy-start | bytes 393220
  7.3 22.3 %all-to-all-start = ((f32[64,512,1]{1,2,0:T(1,128)}), f32[64,512,1]{1,2,0:T(1,128)S(1)}, u32[]{:S(2)}, u32[]{:S(2)}) async-start(f32[64,512,1]{1,2,0:T(1,128)} %bitcast.24), calls=%async_computation | async-start | bytes 262144 | tf_op jit(solution)/shard_map/all_to_all | solution.py:364
  19.0 2.4 %copy-start.5 = (s32[1,1,1,2048]{3,2,1,0:T(1,128)S(1)}, s32[1,1,1,2048]{3,2,1,0:T(1,128)}, u32[]{:S(2)}) copy-start(s32[1,1,1,2048]{3,2,1,0:T(1,128)} %param.17) | copy-start | bytes 24580
  19.1 3.7 %collective-permute-start = (f32[3,1,128]{2,1,0:T(1,128)S(1)}, f32[3,1,128]{2,1,0:T(1,128)S(1)}, u32[]{:S(2)}, u32[]{:S(2)}) collective-permute-start(f32[3,1,128]{2,1,0:T(1,128)S(1)} %bitcast.25), channel_id=1, source_target_pairs={{0,4},{4,0},{8,12},{12,8},{1,5},{5,1},{9,13},{13,9},{2,6},{6,2},{1... | collective-permute-start | bytes 4616 | tf_op jit(solution)/shard_map/ppermute | solution.py:333
  21.4 8.2 %copy-start.3 = (s32[1,1,1,8,2048]{4,3,2,1,0:T(8,128)S(1)}, s32[1,1,1,8,2048]{4,3,2,1,0:T(8,128)}, u32[]{:S(2)}) copy-start(s32[1,1,1,8,2048]{4,3,2,1,0:T(8,128)} %param.18) | copy-start | bytes 196612
  21.4 8.2 %copy-start.4 = (f32[1,1,1,8,2048]{4,3,2,1,0:T(8,128)S(1)}, f32[1,1,1,8,2048]{4,3,2,1,0:T(8,128)}, u32[]{:S(2)}) copy-start(f32[1,1,1,8,2048]{4,3,2,1,0:T(8,128)} %param.19) | copy-start | bytes 196612
  22.7 10.6 %collective-permute-start.1 = (f32[6,1,128]{2,1,0:T(1,128)S(1)}, f32[6,1,128]{2,1,0:T(1,128)S(1)}, u32[]{:S(2)}, u32[]{:S(2)}) collective-permute-start(f32[6,1,128]{2,1,0:T(1,128)S(1)} %constant_dynamic-update-slice_fusion.near_ref), channel_id=1, source_target_pairs={{0,8},{4,12},{8,0},{12,4},{1,9},{5,13},{9,1},{13,5},{2,10},{6,14},... | collective-permute-start | bytes 9224 | tf_op jit(solution)/shard_map/ppermute | solution.py:333
  29.6 10.8 %copy-start.6 = (s32[1,1,1,8]{3,2,1,0:T(1,128)S(1)}, s32[1,1,1,8]{3,2,1,0:T(1,128)}, u32[]{:S(2)}) copy-start(s32[1,1,1,8]{3,2,1,0:T(1,128)} %param.15) | copy-start | bytes 100
  33.3 10.7 %copy-start = (s32[8,32,128]{2,1,0:T(8,128)S(1)}, s32[8,32,128]{2,1,0:T(8,128)}, u32[]{:S(2)}) copy-start(s32[8,32,128]{2,1,0:T(8,128)} %fluid_ref.1) | copy-start | bytes 393220
  33.3 5.8 %collective-permute-start.2 = (f32[256,128]{1,0:T(8,128)S(1)}, f32[256,128]{1,0:T(8,128)S(1)}, u32[]{:S(2)}, u32[]{:S(2)}) collective-permute-start(f32[256,128]{1,0:T(8,128)S(1)} %get-tuple-element.35), channel_id=1, source_target_pairs={{0,16},{16,0},{32,48},{48,32},{64,80},{80,64},{96,112},{112,96},{1... | collective-permute-start | bytes 393224 | tf_op jit(solution)/shard_map/ppermute | solution.py:333
  33.4 8.8 %collective-permute-start.3 = (f32[256,128]{1,0:T(8,128)S(1)}, f32[256,128]{1,0:T(8,128)S(1)}, u32[]{:S(2)}, u32[]{:S(2)}) collective-permute-start(f32[256,128]{1,0:T(8,128)S(1)} %get-tuple-element.37), channel_id=1, source_target_pairs={{0,240},{16,32},{32,16},{48,64},{64,48},{80,96},{96,80},{112,128},... | collective-permute-start | bytes 393224 | tf_op jit(solution)/shard_map/ppermute | solution.py:342
  34.8 7.4 %collective-permute-start.4 = (f32[64,128]{1,0:T(8,128)S(1)}, f32[64,128]{1,0:T(8,128)S(1)}, u32[]{:S(2)}, u32[]{:S(2)}) collective-permute-start(f32[64,128]{1,0:T(8,128)S(1)} %get-tuple-element.38), channel_id=1, source_target_pairs={{0,4},{4,0},{8,12},{12,8},{1,5},{5,1},{9,13},{13,9},{2,6},{6,2},{1... | collective-permute-start | bytes 98312 | tf_op jit(solution)/shard_map/ppermute | solution.py:333
  36.3 5.8 %collective-permute-start.5 = (f32[64,128]{1,0:T(8,128)S(1)}, f32[64,128]{1,0:T(8,128)S(1)}, u32[]{:S(2)}, u32[]{:S(2)}) collective-permute-start(f32[64,128]{1,0:T(8,128)S(1)} %get-tuple-element.39), channel_id=1, source_target_pairs={{0,12},{4,8},{8,4},{12,0},{1,13},{5,9},{9,5},{13,1},{2,14},{6,10},... | collective-permute-start | bytes 98312 | tf_op jit(solution)/shard_map/ppermute | solution.py:342
  38.5 3.7 %collective-permute-start.6 = (f32[16,128]{1,0:T(8,128)S(1)}, f32[16,128]{1,0:T(8,128)S(1)}, u32[]{:S(2)}, u32[]{:S(2)}) collective-permute-start(f32[16,128]{1,0:T(8,128)S(1)} %get-tuple-element.40), channel_id=1, source_target_pairs={{0,1},{1,0},{2,3},{3,2},{4,5},{5,4},{6,7},{7,6},{8,9},{9,8},{10,11... | collective-permute-start | bytes 24584 | tf_op jit(solution)/shard_map/ppermute | solution.py:333
  39.1 4.9 %collective-permute-start.7 = (f32[16,128]{1,0:T(8,128)S(1)}, f32[16,128]{1,0:T(8,128)S(1)}, u32[]{:S(2)}, u32[]{:S(2)}) collective-permute-start(f32[16,128]{1,0:T(8,128)S(1)} %get-tuple-element.41), channel_id=1, source_target_pairs={{0,3},{1,2},{2,1},{3,0},{4,7},{5,6},{6,5},{7,4},{8,11},{9,10},{10,... | collective-permute-start | bytes 24584 | tf_op jit(solution)/shard_map/ppermute | solution.py:342

commit v5 on v3

--- a/solution.py
+++ b/solution.py
@@ -59,16 +59,16 @@
     vel_hbm, nu_hbm, rows_hbm, out_ref, table_ref, vel_ref, nu_ref, rows_ref, turn_ref, sems
 ):
     copies = [
-        pltpu.make_async_copy(vel_hbm, vel_ref, sems.at[0]),
-        pltpu.make_async_copy(nu_hbm, nu_ref, sems.at[1]),
-        pltpu.make_async_copy(rows_hbm, rows_ref, sems.at[2]),
+        pltpu.make_async_copy(vel_hbm.at[0], vel_ref.at[0], sems.at[0]),
+        pltpu.make_async_copy(vel_hbm.at[1], vel_ref.at[1], sems.at[1]),
+        pltpu.make_async_copy(vel_hbm.at[2], vel_ref.at[2], sems.at[2]),
+        pltpu.make_async_copy(nu_hbm, nu_ref, sems.at[3]),
+        pltpu.make_async_copy(rows_hbm, rows_ref, sems.at[4]),
     ]
     for copy in copies:
         copy.start()
-    copies[0].wait()
     for f in range(4):
-        if f == 3:
-            copies[1].wait()
+        copies[f].wait()
         block = vel_ref[f] if f < 3 else nu_ref[...]
         for half in range(2):
             turn_ref[half, pl.ds(f, CZ, stride=4), :] = block[half * 128:half * 128 + 128].T
@@ -76,7 +76,7 @@
         high, low = in_two(turn_ref[half])
         table_ref[:, half * 128:half * 128 + 128] = high
         table_ref[:, ROWS + half * 128:ROWS + half * 128 + 128] = low
-    copies[2].wait()
+    copies[4].wait()
     top = lax.broadcasted_iota(i32, (8, 128), 0) < 4
 
     def step(pair, carry):
@@ -356,7 +356,7 @@
         pack_kernel, shape(256, 128), [anywhere()] * 3,
         [pltpu.VMEM((512, 2 * ROWS), bf16),
          pltpu.VMEM((3, ROWS, CZ), f32), pltpu.VMEM((ROWS, CZ), f32), pltpu.VMEM((64, 128), i32),
-         pltpu.VMEM((2, 512, 128), f32), pltpu.SemaphoreType.DMA((3,))],
+         pltpu.VMEM((2, 512, 128), f32), pltpu.SemaphoreType.DMA((5,))],
         "pack_rows", 4_000_000_000, 1_000_000, 60 * 1024 * 1024,
     )(vel, nu, rows)
     points, outgoing = lax.optimization_barrier((surface.reshape(3, 1, 128), outgoing))

time: 46.2 us -> 46.1 us (level)
  waiting for transfers between devices: 5.5 us -> 6.24 us
  Pallas kernels: 15.2 us -> 14.5 us
    ppermute x3, waiting for transfers between devices: 0.34 us -> 1.08 us  [swap_down(): lax.ppermute(block, axis, [(i, (i + (1 if i % 2 else -1)) % count) for i...]
    pallas_call x1, Pallas kernels: 2.55 us -> 1.81 us  [on_device(): call(wall_kernel, (shape(32, TY, CZ), shape(32, TY, CZ)), [vmem()] * 4, [...]
  transfers between devices with their start and end apart: 9 -> 9, of which waited for: 3 -> 3; matrix products, arithmetic and copies ran while one was open for 0% -> 0% of each run, Pallas kernels for 15% -> 13%
where the time goes in v5:
time: 46.1 us; the launch traced here: 45.9 us
  starting transfers between devices  23.6 us (51%)
  Pallas kernels  14.5 us (31%)
  waiting for transfers between devices  6.24 us (14%)
  between operations  1.43 us (3%)
    all_to_all x1, starting transfers between devices, on_device(): lax.all_to_all(outgoing.reshape(256 * 128), ('gx', 'gz'), split_axis=0, c...  11.7 us
    ppermute x5, starting transfers between devices, exchange(): return lax.ppermute(block, axis, [(i, i ^ bit) for i in range(count)])  7.07 us
    pallas_call x1, Pallas kernels, on_device(): call(pack_kernel, shape(256, 128), [anywhere()] * 3, [pltpu.VMEM((512, 2...  6.68 us
    ppermute x3, starting transfers between devices, swap_down(): lax.ppermute(block, axis, [(i, (i + (1 if i % 2 else -1)) % count) for i...  4.85 us
    pallas_call x1, Pallas kernels, on_device(): call(fill_kernel, (shape(4, ROWS, CZ), shape(256, 128), shape(256, 128),...  3.68 us
    all_to_all x1, waiting for transfers between devices, on_device(): lax.all_to_all(outgoing.reshape(256 * 128), ('gx', 'gz'), split_axis=0, c...  3.66 us
    pallas_call x1, Pallas kernels, on_device(): call(advance_kernel, (shape(3, CX, CY, CZ), shape(CX, CY, CZ)), [vmem()]...  1.88 us
    pallas_call x1, Pallas kernels, on_device(): call(wall_kernel, (shape(32, TY, CZ), shape(32, TY, CZ)), [vmem()] * 4, [...  1.81 us
  transfers between devices with their start and end apart: 9, of which 3 were waited for; matrix products, arithmetic and copies ran while one was open for 0% of the time, Pallas kernels for 13%

profile of v5, /device:TPU:32, one launch (start us, length us, event | category | flops | bytes accessed | tf_op | source)
XLA Modules:
  0.0 45.9 jit_solution(11594361583967874389)
XLA Ops:
  0.6 6.7 %pack_rows.1 = f32[256,128]{1,0:T(8,128)} custom-call(f32[3,256,128]{2,1,0:T(8,128)} %bitcast.16, f32[256,128]{1,0:T(8,128)} %bitcast.18, s32[64,128]{1,0:T(8,128)} %bitcast.27), custom_call_target="tpu_custom_call" | custom-call | flops 4000000000 | bytes 1000000 | tf_op jit(solution)/shard_map/pack_rows/pallas_call | solution.py:355
  7.3 0.0 copy-start.7
  7.3 0.0 copy-start.2
  7.4 0.0 copy-start.5
  7.4 11.7 %all-to-all-start = ((f32[64,512,1]{1,2,0:T(1,128)}), f32[64,512,1]{1,2,0:T(1,128)S(1)}, u32[]{:S(2)}, u32[]{:S(2)}) async-start(f32[64,512,1]{1,2,0:T(1,128)} %bitcast.24), calls=%async_computation | async-start | bytes 262144 | tf_op jit(solution)/shard_map/all_to_all | solution.py:363
  19.1 1.7 %collective-permute-start = (f32[3,1,128]{2,1,0:T(1,128)S(1)}, f32[3,1,128]{2,1,0:T(1,128)S(1)}, u32[]{:S(2)}, u32[]{:S(2)}) collective-permute-start(f32[3,1,128]{2,1,0:T(1,128)S(1)} %bitcast.25), channel_id=1, source_target_pairs={{0,4},{4,0},{8,12},{12,8},{1,5},{5,1},{9,13},{13,9},{2,6},{6,2},{1... | collective-permute-start | bytes 4616 | tf_op jit(solution)/shard_map/ppermute | solution.py:332
  20.8 0.0 copy-start.3
  20.8 0.0 copy-start.4
  20.8 0.5 %prepare.1 = (f32[4,256,128]{2,1,0:T(8,128)S(1)}, bf16[256,2048]{1,0:T(8,128)(2,1)S(1)}, bf16[128,2048]{1,0:T(8,128)(2,1)S(1)}) custom-call(f32[3,256,128]{2,1,0:T(8,128)S(1)} %bitcast.17, f32[256,128]{1,0:T(8,128)S(1)} %bitcast.19, s32[16,128]{1,0:T(8,128)S(1)} %bitcast.22), custom_call_target="tpu_custom_call" | custom-call | flops 200000000 | bytes 2000000 | tf_op jit(solution)/shard_map/prepare/pallas_call | solution.py:369
  21.3 1.5 %collective-permute-done = f32[3,1,128]{2,1,0:T(1,128)S(1)} collective-permute-done((f32[3,1,128]{2,1,0:T(1,128)S(1)}, f32[3,1,128]{2,1,0:T(1,128)S(1)}, u32[]{:S(2)}, u32[]{:S(2)}) %collective-permute-start) | collective-permute-done | bytes 1568 | tf_op jit(solution)/shard_map/ppermute | solution.py:332
  22.8 3.2 %collective-permute-start.1 = (f32[6,1,128]{2,1,0:T(1,128)S(1)}, f32[6,1,128]{2,1,0:T(1,128)S(1)}, u32[]{:S(2)}, u32[]{:S(2)}) collective-permute-start(f32[6,1,128]{2,1,0:T(1,128)S(1)} %constant_dynamic-update-slice_fusion.near_ref), channel_id=1, source_target_pairs={{0,8},{4,12},{8,0},{12,4},{1,9},{5,13},{9,1},{13,5},{2,10},{6,14},... | collective-permute-start | bytes 9224 | tf_op jit(solution)/shard_map/ppermute | solution.py:332
  26.0 3.7 %all-to-all-done = f32[64,512,1]{1,2,0:T(1,128)S(1)} async-done(((f32[64,512,1]{1,2,0:T(1,128)}), f32[64,512,1]{1,2,0:T(1,128)S(1)}, u32[]{:S(2)}, u32[]{:S(2)}) %all-to-all-start) | async-done | bytes 131104 | tf_op jit(solution)/shard_map/all_to_all | solution.py:363
  29.7 3.7 %fill_ghosts.1 = (f32[4,256,128]{2,1,0:T(8,128)S(1)}, f32[256,128]{1,0:T(8,128)S(1)}, f32[256,128]{1,0:T(8,128)S(1)}, f32[64,128]{1,0:T(8,128)S(1)}, f32[64,128]...) custom-call(f32[256,128]{1,0:T(8,128)S(1)} %bitcast.15, s32[8,2048]{1,0:T(8,128)S(1)} %bitcast.20, ...), custom_call_target="tpu_custom_call" | custom-call | flops 4000000000 | bytes 2000000 | tf_op jit(solution)/shard_map/fill_ghosts/pallas_call | solution.py:376
  33.3 0.0 copy-start
  33.4 0.0 collective-permute-done.1.far_ref
  33.4 0.1 collective-permute-start.2
  33.5 1.4 %collective-permute-start.3 = (f32[256,128]{1,0:T(8,128)S(1)}, f32[256,128]{1,0:T(8,128)S(1)}, u32[]{:S(2)}, u32[]{:S(2)}) collective-permute-start(f32[256,128]{1,0:T(8,128)S(1)} %get-tuple-element.36), channel_id=1, source_target_pairs={{0,240},{16,32},{32,16},{48,64},{64,48},{80,96},{96,80},{112,128},... | collective-permute-start | bytes 393224 | tf_op jit(solution)/shard_map/ppermute | solution.py:341
  34.8 1.6 %collective-permute-start.4 = (f32[64,128]{1,0:T(8,128)S(1)}, f32[64,128]{1,0:T(8,128)S(1)}, u32[]{:S(2)}, u32[]{:S(2)}) collective-permute-start(f32[64,128]{1,0:T(8,128)S(1)} %get-tuple-element.37), channel_id=1, source_target_pairs={{0,4},{4,0},{8,12},{12,8},{1,5},{5,1},{9,13},{13,9},{2,6},{6,2},{1... | collective-permute-start | bytes 98312 | tf_op jit(solution)/shard_map/ppermute | solution.py:332
  36.4 2.2 %collective-permute-start.5 = (f32[64,128]{1,0:T(8,128)S(1)}, f32[64,128]{1,0:T(8,128)S(1)}, u32[]{:S(2)}, u32[]{:S(2)}) collective-permute-start(f32[64,128]{1,0:T(8,128)S(1)} %get-tuple-element.38), channel_id=1, source_target_pairs={{0,12},{4,8},{8,4},{12,0},{1,13},{5,9},{9,5},{13,1},{2,14},{6,10},... | collective-permute-start | bytes 98312 | tf_op jit(solution)/shard_map/ppermute | solution.py:341
  38.6 0.5 %collective-permute-start.6 = (f32[16,128]{1,0:T(8,128)S(1)}, f32[16,128]{1,0:T(8,128)S(1)}, u32[]{:S(2)}, u32[]{:S(2)}) collective-permute-start(f32[16,128]{1,0:T(8,128)S(1)} %get-tuple-element.39), channel_id=1, source_target_pairs={{0,1},{1,0},{2,3},{3,2},{4,5},{5,4},{6,7},{7,6},{8,9},{9,8},{10,11... | collective-permute-start | bytes 24584 | tf_op jit(solution)/shard_map/ppermute | solution.py:332
  39.1 1.3 %collective-permute-start.7 = (f32[16,128]{1,0:T(8,128)S(1)}, f32[16,128]{1,0:T(8,128)S(1)}, u32[]{:S(2)}, u32[]{:S(2)}) collective-permute-start(f32[16,128]{1,0:T(8,128)S(1)} %get-tuple-element.40), channel_id=1, source_target_pairs={{0,3},{1,2},{2,1},{3,0},{4,7},{5,6},{6,5},{7,4},{8,11},{9,10},{10,... | collective-permute-start | bytes 24584 | tf_op jit(solution)/shard_map/ppermute | solution.py:341
  41.1 1.8 %wall.1 = (f32[32,8,128]{2,1,0:T(8,128)}, f32[32,8,128]{2,1,0:T(8,128)S(1)}) custom-call(s32[1,8]{1,0:T(1,128)S(1)} %bitcast.23, f32[1,1]{1,0:T(1,128)} %bitcast.13.pitch_ref, f32[6,1,128]{2,1,0:T(1,128)S(1)} %constant_dynamic-update-slice_fusion.near_ref, f32[6,1,128]{2,1,0:T(1,128)S(1)} %collective-permute-done.1.far_ref), custom_call_target="tpu_custom_call" | custom-call | flops 30000000 | bytes 200000 | tf_op jit(solution)/shard_map/wall/pallas_call | solution.py:387
  42.9 1.1 %collective-permute-done.7.z2_ref = f32[16,128]{1,0:T(8,128)S(1)} collective-permute-done((f32[16,128]{1,0:T(8,128)S(1)}, f32[16,128]{1,0:T(8,128)S(1)}, u32[]{:S(2)}, u32[]{:S(2)}) %collective-permute-start.7) | collective-permute-done | bytes 8224 | tf_op jit(solution)/shard_map/ppermute | solution.py:341
  44.0 1.9 %advance.1 = (f32[3,8,32,128]{3,2,1,0:T(8,128)}, f32[8,32,128]{2,1,0:T(8,128)}) custom-call(f32[4,256,128]{2,1,0:T(8,128)S(1)} %get-tuple-element.31.filled_ref, f32[256,128]{1,0:T(8,128)S(1)} %collective-permute-done.2.x1_ref, f32[256,128]{1,0:T(8,128)S(1)} %collective-permute-done.3.x2_ref, f32[64,128]{1,0:T(8,128)S(1)} %collective-permute-done.4.y1_ref, ...), custom_call_target="tpu_custom_call" | custom-call | flops 20000000 | bytes 3000000 | tf_op jit(solution)/shard_map/advance/pallas_call | solution.py:399
  (17 shorter events, 0.0 us)
Async XLA Ops:
  0.6 20.2 %copy-start.1 = (f32[3,8,32,128]{3,2,1,0:T(8,128)S(1)}, f32[3,8,32,128]{3,2,1,0:T(8,128)}, u32[]{:S(2)}) copy-start(f32[3,8,32,128]{3,2,1,0:T(8,128)} %param.10) | copy-start | bytes 1179652
  7.3 11.8 %copy-start.7 = (f32[1,1,3,128]{3,1,2,0:T(1,128)S(1)}, f32[1,1,3,128]{3,1,2,0:T(1,128)}, u32[]{:S(2)}) copy-start(f32[1,1,3,128]{3,1,2,0:T(1,128)} %param.13) | copy-start | bytes 4612
  7.3 13.4 %copy-start.2 = (f32[8,32,128]{2,1,0:T(8,128)S(1)}, f32[8,32,128]{2,1,0:T(8,128)}, u32[]{:S(2)}) copy-start(f32[8,32,128]{2,1,0:T(8,128)} %param.11) | copy-start | bytes 393220
  7.4 13.4 %copy-start.5 = (s32[1,1,1,2048]{3,2,1,0:T(1,128)S(1)}, s32[1,1,1,2048]{3,2,1,0:T(1,128)}, u32[]{:S(2)}) copy-start(s32[1,1,1,2048]{3,2,1,0:T(1,128)} %param.17) | copy-start | bytes 24580
  7.4 22.3 %all-to-all-start = ((f32[64,512,1]{1,2,0:T(1,128)}), f32[64,512,1]{1,2,0:T(1,128)S(1)}, u32[]{:S(2)}, u32[]{:S(2)}) async-start(f32[64,512,1]{1,2,0:T(1,128)} %bitcast.24), calls=%async_computation | async-start | bytes 262144 | tf_op jit(solution)/shard_map/all_to_all | solution.py:363
  19.1 3.7 %collective-permute-start = (f32[3,1,128]{2,1,0:T(1,128)S(1)}, f32[3,1,128]{2,1,0:T(1,128)S(1)}, u32[]{:S(2)}, u32[]{:S(2)}) collective-permute-start(f32[3,1,128]{2,1,0:T(1,128)S(1)} %bitcast.25), channel_id=1, source_target_pairs={{0,4},{4,0},{8,12},{12,8},{1,5},{5,1},{9,13},{13,9},{2,6},{6,2},{1... | collective-permute-start | bytes 4616 | tf_op jit(solution)/shard_map/ppermute | solution.py:332
  20.8 8.9 %copy-start.3 = (s32[1,1,1,8,2048]{4,3,2,1,0:T(8,128)S(1)}, s32[1,1,1,8,2048]{4,3,2,1,0:T(8,128)}, u32[]{:S(2)}) copy-start(s32[1,1,1,8,2048]{4,3,2,1,0:T(8,128)} %param.18) | copy-start | bytes 196612
  20.8 8.8 %copy-start.4 = (f32[1,1,1,8,2048]{4,3,2,1,0:T(8,128)S(1)}, f32[1,1,1,8,2048]{4,3,2,1,0:T(8,128)}, u32[]{:S(2)}) copy-start(f32[1,1,1,8,2048]{4,3,2,1,0:T(8,128)} %param.19) | copy-start | bytes 196612
  22.8 10.6 %collective-permute-start.1 = (f32[6,1,128]{2,1,0:T(1,128)S(1)}, f32[6,1,128]{2,1,0:T(1,128)S(1)}, u32[]{:S(2)}, u32[]{:S(2)}) collective-permute-start(f32[6,1,128]{2,1,0:T(1,128)S(1)} %constant_dynamic-update-slice_fusion.near_ref), channel_id=1, source_target_pairs={{0,8},{4,12},{8,0},{12,4},{1,9},{5,13},{9,1},{13,5},{2,10},{6,14},... | collective-permute-start | bytes 9224 | tf_op jit(solution)/shard_map/ppermute | solution.py:332
  29.7 11.4 %copy-start.6 = (s32[1,1,1,8]{3,2,1,0:T(1,128)S(1)}, s32[1,1,1,8]{3,2,1,0:T(1,128)}, u32[]{:S(2)}) copy-start(s32[1,1,1,8]{3,2,1,0:T(1,128)} %param.15) | copy-start | bytes 100
  33.3 10.7 %copy-start = (s32[8,32,128]{2,1,0:T(8,128)S(1)}, s32[8,32,128]{2,1,0:T(8,128)}, u32[]{:S(2)}) copy-start(s32[8,32,128]{2,1,0:T(8,128)} %fluid_ref.1) | copy-start | bytes 393220
  33.4 5.8 %collective-permute-start.2 = (f32[256,128]{1,0:T(8,128)S(1)}, f32[256,128]{1,0:T(8,128)S(1)}, u32[]{:S(2)}, u32[]{:S(2)}) collective-permute-start(f32[256,128]{1,0:T(8,128)S(1)} %get-tuple-element.34), channel_id=1, source_target_pairs={{0,16},{16,0},{32,48},{48,32},{64,80},{80,64},{96,112},{112,96},{1... | collective-permute-start | bytes 393224 | tf_op jit(solution)/shard_map/ppermute | solution.py:332
  33.5 9.5 %collective-permute-start.3 = (f32[256,128]{1,0:T(8,128)S(1)}, f32[256,128]{1,0:T(8,128)S(1)}, u32[]{:S(2)}, u32[]{:S(2)}) collective-permute-start(f32[256,128]{1,0:T(8,128)S(1)} %get-tuple-element.36), channel_id=1, source_target_pairs={{0,240},{16,32},{32,16},{48,64},{64,48},{80,96},{96,80},{112,128},... | collective-permute-start | bytes 393224 | tf_op jit(solution)/shard_map/ppermute | solution.py:341
  34.8 8.1 %collective-permute-start.4 = (f32[64,128]{1,0:T(8,128)S(1)}, f32[64,128]{1,0:T(8,128)S(1)}, u32[]{:S(2)}, u32[]{:S(2)}) collective-permute-start(f32[64,128]{1,0:T(8,128)S(1)} %get-tuple-element.37), channel_id=1, source_target_pairs={{0,4},{4,0},{8,12},{12,8},{1,5},{5,1},{9,13},{13,9},{2,6},{6,2},{1... | collective-permute-start | bytes 98312 | tf_op jit(solution)/shard_map/ppermute | solution.py:332
  36.4 6.5 %collective-permute-start.5 = (f32[64,128]{1,0:T(8,128)S(1)}, f32[64,128]{1,0:T(8,128)S(1)}, u32[]{:S(2)}, u32[]{:S(2)}) collective-permute-start(f32[64,128]{1,0:T(8,128)S(1)} %get-tuple-element.38), channel_id=1, source_target_pairs={{0,12},{4,8},{8,4},{12,0},{1,13},{5,9},{9,5},{13,1},{2,14},{6,10},... | collective-permute-start | bytes 98312 | tf_op jit(solution)/shard_map/ppermute | solution.py:341
  38.6 4.3 %collective-permute-start.6 = (f32[16,128]{1,0:T(8,128)S(1)}, f32[16,128]{1,0:T(8,128)S(1)}, u32[]{:S(2)}, u32[]{:S(2)}) collective-permute-start(f32[16,128]{1,0:T(8,128)S(1)} %get-tuple-element.39), channel_id=1, source_target_pairs={{0,1},{1,0},{2,3},{3,2},{4,5},{5,4},{6,7},{7,6},{8,9},{9,8},{10,11... | collective-permute-start | bytes 24584 | tf_op jit(solution)/shard_map/ppermute | solution.py:332
  39.1 4.9 %collective-permute-start.7 = (f32[16,128]{1,0:T(8,128)S(1)}, f32[16,128]{1,0:T(8,128)S(1)}, u32[]{:S(2)}, u32[]{:S(2)}) collective-permute-start(f32[16,128]{1,0:T(8,128)S(1)} %get-tuple-element.40), channel_id=1, source_target_pairs={{0,3},{1,2},{2,1},{3,0},{4,7},{5,6},{6,5},{7,4},{8,11},{9,10},{10,... | collective-permute-start | bytes 24584 | tf_op jit(solution)/shard_map/ppermute | solution.py:341
